TPU v7x, 32 devices: a whole 2x2x4 slice. The times are simulated.
32 devices in a mesh: section: 2 (over core), dp: 2 (over y), ctx: 2 (over x), tp: 4 (over z).
Axes of the slice: x: 2, y: 2, z: 4, core: 2. Of those that a mesh axis runs over, the one named last changes fastest.
Arguments:
- acts: bfloat16 [4, 2, 2048, 1024], P(None, 'dp', 'ctx'), may hold values from -6 to 6
- cotangent: float32 [4, 2, 2048, 1024], P(None, 'dp', 'ctx'), may hold values from -6 to 6
- lengths: int32 [4, 2], P(None, 'dp'), may hold values from 1024 to 2048, as said below
- norm_gain: bfloat16 [2, 1024], P('section', ('dp', 'ctx')), may hold values from 0.099609375 to 1.8984375
- proj_gate_x: bfloat16 [2, 1024, 2, 2048], P('section', ('dp', 'ctx'), None, 'tp'), may hold values from -0.1875 to 0.1875
- proj_state: bfloat16 [2, 1024, 256], P('section', ('dp', 'ctx')), may hold values from -0.1875 to 0.1875
- proj_step: bfloat16 [2, 1024, 32], P('section', ('dp', 'ctx'), 'tp'), may hold values from -0.1875 to 0.1875
- conv_inner: float32 [2, 5, 2048], P('section', None, 'tp'), may hold values from -3 to 3
- conv_state: float32 [2, 5, 256], P('section'), may hold values from -3 to 3
- step_bias: float32 [2, 32], P('section', 'tp'), may hold values from -10 to -2
- decay_log: float32 [2, 32], P('section', 'tp'), may hold values from -1 to 2
- skip_weight: float32 [2, 32], P('section', 'tp'), may hold values from 0.5 to 1.5
- out_gain: float32 [2, 2048], P('section', 'tp'), may hold values from 0.1 to 1.9
- proj_out: bfloat16 [2, 2048, 1024], P('section', 'tp', ('dp', 'ctx')), may hold values from -0.125 to 0.125
Outputs:
- section_out: bfloat16 [2, 4, 2, 2048, 1024], P('section', None, 'dp', ('ctx', 'tp'))
- input_grad: float32 [2, 4, 2, 2048, 1024], P('section', None, 'dp', ('ctx', 'tp'))
- grad_norm_gain: float32 [2, 1024], P('section', ('dp', 'ctx'))
- grad_gate_x: float32 [2, 1024, 2, 2048], P('section', ('dp', 'ctx'), None, 'tp')
- grad_state: float32 [2, 1024, 256], P('section', ('dp', 'ctx'))
- grad_step: float32 [2, 1024, 32], P('section', ('dp', 'ctx'), 'tp')
- grad_conv_inner: float32 [2, 5, 2048], P('section', None, 'tp')
- grad_conv_state: float32 [2, 5, 256], P('section')
- grad_step_bias: float32 [2, 32], P('section', 'tp')
- grad_decay_log: float32 [2, 32], P('section', 'tp')
- grad_skip: float32 [2, 32], P('section', 'tp')
- grad_out_gain: float32 [2, 2048], P('section', 'tp')
- grad_out: float32 [2, 2048, 1024], P('section', 'tp', ('dp', 'ctx'))
Inputs may be any that keep to these rules, and one draw needn't show every extreme that they name: `lengths`: every data rank has, in one of its 4 micro-batches drawn from the seed, a sequence that fills all 2048 positions of its row.
All inputs are finite; a program needn't handle non-finite values.
Results may differ from a plain program's by a relative error of at most 0.024.
Values may be sent and summed in bfloat16 or wider, within the bound.
No kernel may reach another device: no remote copies, remote signals or barrier semaphores. Data moves between devices by JAX's collectives and lax.ppermute only.
A program may use at most 384 MiB of HBM per device.

v0:
```python
import functools

import jax
import jax.numpy as jnp
from jax import lax
from jax.experimental import pallas as pl
from jax.experimental.pallas import tpu as pltpu
from jax.sharding import PartitionSpec as P

HEADDIM = 64
STATE = 128
INNER = 2048
CONV = 4
CHUNK = 128
LANES = 128
RIM = 16

highest = lax.Precision.HIGHEST
epsilon = 1e-05
low = jnp.bfloat16
full = jnp.float32


def dot_nn(a, b, precision=None):
    return lax.dot_general(
        a, b, (((1,), (0,)), ((), ())), precision=precision, preferred_element_type=full
    )


def dot_nt(a, b, precision=None):
    return lax.dot_general(
        a, b, (((1,), (1,)), ((), ())), precision=precision, preferred_element_type=full
    )


def dot_tn(a, b, precision=None):
    return lax.dot_general(
        a, b, (((0,), (0,)), ((), ())), precision=precision, preferred_element_type=full
    )


def shifted(value, axis, steps):
    count = lax.axis_size(axis)
    first, last = (max(0, -steps), min(count, count - steps))
    return lax.ppermute(value, axis, [(source, source + steps) for source in range(first, last)])


def rotated(value, axis, steps):
    count = lax.axis_size(axis)
    return lax.ppermute(value, axis, [(i, (i + steps) % count) for i in range(count)])


def line_gather(value, axis, dim=0):
    count = lax.axis_size(axis)
    place = lax.axis_index(axis)
    if count == 1:
        return jnp.expand_dims(value, dim)
    if count == 2:
        other = rotated(value, axis, 1)
        first = place == 0
        return jnp.stack([jnp.where(first, value, other), jnp.where(first, other, value)], axis=dim)
    up = down = value
    before, after = [], []
    for _ in range(1, count):
        up = shifted(up, axis, 1)
        down = shifted(down, axis, -1)
        before.insert(0, up)
        after.append(down)
    line = jnp.stack(before + [value] + after, axis=dim)
    return lax.dynamic_slice_in_dim(line, count - 1 - place, count, dim)


def ring_gather(value, axis):
    count = lax.axis_size(axis)
    place = lax.axis_index(axis)
    came = [value] + [rotated(value, axis, steps) for steps in range(1, count)]
    line = jnp.stack(came[::-1] + came[:0:-1])
    return lax.dynamic_slice_in_dim(line, count - 1 - place, count, 0)


def scatter_sum(pick, axis):
    count = lax.axis_size(axis)
    place = lax.axis_index(axis)
    total = pick(place).astype(full)
    for steps in range(1, count):
        total = total + rotated(pick((place + steps) % count), axis, steps).astype(full)
    return total


def all_sum(value, axis):
    total = value
    for steps in range(1, lax.axis_size(axis)):
        total = total + rotated(value, axis, steps)
    return total


def swap_cores(value):
    return lax.ppermute(value, "section", [(0, 1), (1, 0)])


def spread_rows(value, pairs_of):
    count = lax.axis_size("tp")
    place = lax.axis_index("tp")
    result = jnp.zeros_like(value)
    own = lax.dynamic_index_in_dim(value, place, 0, False)
    result = lax.dynamic_update_index_in_dim(result, own, place, 0)
    for steps in range(1, count):
        block = lax.dynamic_index_in_dim(value, (place + steps) % count, 0, False)
        pairs = [
            (core * count + i, core * count + (i + steps) % count)
            for core in pairs_of
            for i in range(count)
        ]
        arrived = lax.ppermute(block, ("section", "tp"), pairs)
        result = lax.dynamic_update_index_in_dim(result, arrived, (place - steps) % count, 0)
    return result


def gather_rows(early, late):
    width = early.shape[-1]
    half_a = line_gather(line_gather(early, "ctx"), "dp").reshape(-1, width)
    half_b = line_gather(line_gather(late, "dp"), "ctx", 1).reshape(-1, width)
    return half_a, half_b


def columns(pieces):
    return jnp.concatenate(list(pieces), axis=-1)


def as_rows(vector, width):
    rows = -(-vector.shape[0] // (16 * width)) * 16
    return jnp.pad(vector, (0, rows * width - vector.shape[0])).reshape(rows, width)


def tied(value, other):
    return lax.optimization_barrier((value, other))


def conv_taps_sum(taps_ref, rows_of):
    total = taps_ref[CONV : CONV + 1, :]
    for k in range(CONV):
        total = total + taps_ref[k : k + 1, :] * rows_of(k)
    return total


def prep_kernel(
    feed_ref, rim_ref, taps_ref, raw_ref, bias_ref, rate_ref,
    act_ref, dt_ref, cum_ref, cumt_ref, since_ref, local_ref,
    window, run,
):
    inner = local_ref.shape[0]

    @pl.when(pl.program_id(0) == 0)
    def _():
        window[:RIM, :] = rim_ref[...].astype(full)
        run[...] = jnp.zeros_like(run)
        local_ref[...] = jnp.zeros_like(local_ref)

    window[RIM:, :] = feed_ref[...].astype(full)
    pre = conv_taps_sum(taps_ref, lambda k: window[RIM - CONV + 1 + k : RIM - CONV + 1 + k + CHUNK, :])
    act = pre * jax.nn.sigmoid(pre)
    act_ref[...] = act
    window[:RIM, :] = window[CHUNK:, :]
    raw = raw_ref[...] + bias_ref[...]
    dt = jnp.maximum(raw, 0.0) + jnp.log1p(jnp.exp(-jnp.abs(raw)))
    row = lax.broadcasted_iota(jnp.int32, (CHUNK, CHUNK), 0)
    col = lax.broadcasted_iota(jnp.int32, (CHUNK, CHUNK), 1)
    cum = dot_nn((row >= col).astype(full), rate_ref[...] * dt, highest)
    dt_ref[...] = dt
    cum_ref[...] = cum
    cumt_ref[...] = cum.T[: cumt_ref.shape[0]]
    since_ref[...] = jnp.exp(run[0:1, :] + cum)
    end = cum[CHUNK - 1 : CHUNK, :]
    run[...] = run[...] + end
    weight = jnp.exp(end - cum) * dt
    shrink = jnp.exp(end)
    left = col < HEADDIM
    upper = row < HEADDIM
    b_low = act[:, inner : inner + STATE].astype(low)
    for pair in range(inner // LANES):
        h0, h1 = 2 * pair, 2 * pair + 1
        span = slice(pair * LANES, (pair + 1) * LANES)
        each = jnp.where(left, weight[:, h0 : h0 + 1], weight[:, h1 : h1 + 1])
        fresh = dot_tn((act[:, span] * each).astype(low), b_low)
        keep = jnp.where(upper, shrink[:, h0 : h0 + 1], shrink[:, h1 : h1 + 1])
        local_ref[span, :] = keep * local_ref[span, :] + fresh


def mixer_prep(feed, rim, taps, raw, bias, rate, heads):
    rows, channels = feed.shape
    inner = heads * HEADDIM
    lanes = pl.BlockSpec((CHUNK, LANES), lambda i: (i, 0))
    lane_row = pl.BlockSpec((1, LANES), lambda i: (0, 0))
    by_lane = jax.ShapeDtypeStruct((rows, LANES), full)
    return pl.pallas_call(
        prep_kernel,
        grid=(rows // CHUNK,),
        in_specs=[
            pl.BlockSpec((CHUNK, channels), lambda i: (i, 0)),
            pl.BlockSpec((RIM, channels), lambda i: (0, 0)),
            pl.BlockSpec((8, channels), lambda i: (0, 0)),
            lanes,
            lane_row,
            lane_row,
        ],
        out_specs=[
            pl.BlockSpec((CHUNK, channels), lambda i: (i, 0)),
            lanes,
            lanes,
            pl.BlockSpec((heads, CHUNK), lambda i: (0, i)),
            lanes,
            pl.BlockSpec((inner, STATE), lambda i: (0, 0)),
        ],
        out_shape=[
            jax.ShapeDtypeStruct((rows, channels), full),
            by_lane,
            by_lane,
            jax.ShapeDtypeStruct((heads, rows), full),
            by_lane,
            jax.ShapeDtypeStruct((inner, STATE), full),
        ],
        scratch_shapes=[pltpu.VMEM((CHUNK + RIM, channels), full), pltpu.VMEM((8, LANES), full)],
        compiler_params=pltpu.CompilerParams(
            dimension_semantics=("arbitrary",), vmem_limit_bytes=40 * 1024 * 1024
        ),
        cost_estimate=pl.CostEstimate(
            flops=rows * inner * 2 * STATE, bytes_accessed=rows * channels * 6, transcendentals=rows * channels
        ),
        name="mixer_prep",
    )(feed, rim, taps, raw, bias, rate)


def fwd_kernel(x_ref, bc_ref, dt_ref, cum_ref, cumt_ref, skip_ref, enter_ref, y_ref, start_ref, state):
    @pl.when(pl.program_id(0) == 0)
    def _():
        state[...] = enter_ref[...].astype(full)

    heads = cumt_ref.shape[0]
    start_ref[0] = state[...].astype(low)
    b_low = bc_ref[:, :STATE].astype(low)
    c_low = bc_ref[:, STATE:].astype(low)
    row = lax.broadcasted_iota(jnp.int32, (CHUNK, CHUNK), 0)
    col = lax.broadcasted_iota(jnp.int32, (CHUNK, CHUNK), 1)
    left = col < HEADDIM
    upper = row < HEADDIM
    masked = jnp.where(row >= col, dot_nt(c_low, b_low), 0.0)
    for pair in range(heads // 2):
        h0, h1 = 2 * pair, 2 * pair + 1
        span = slice(pair * LANES, (pair + 1) * LANES)
        cum0 = jnp.broadcast_to(cum_ref[:, h0 : h0 + 1], (CHUNK, CHUNK))
        cum1 = jnp.broadcast_to(cum_ref[:, h1 : h1 + 1], (CHUNK, CHUNK))
        w0 = jnp.exp(jnp.minimum(cum0 - cumt_ref[h0 : h0 + 1, :], 0.0)) * masked
        w1 = jnp.exp(jnp.minimum(cum1 - cumt_ref[h1 : h1 + 1, :], 0.0)) * masked
        weights = jnp.concatenate([w0.astype(low), w1.astype(low)], axis=1)
        x_pair = x_ref[:, span]
        u = x_pair * jnp.where(left, dt_ref[:, h0 : h0 + 1], dt_ref[:, h1 : h1 + 1])
        u_low = u.astype(low)
        zero = jnp.zeros_like(u_low)
        u_both = jnp.concatenate([jnp.where(left, u_low, zero), jnp.where(left, zero, u_low)], axis=0)
        cum_pair = jnp.where(left, cum0, cum1)
        s_pair = state[span, :]
        carried = jnp.exp(cum_pair) * dot_nt(c_low, s_pair.astype(low))
        y_ref[:, span] = dot_nn(weights, u_both) + carried + skip_ref[:, span] * x_pair
        end0 = cum_ref[CHUNK - 1 : CHUNK, h0 : h0 + 1]
        end1 = cum_ref[CHUNK - 1 : CHUNK, h1 : h1 + 1]
        ahead = jnp.exp(jnp.where(left, end0, end1) - cum_pair)
        fresh = dot_tn((u * ahead).astype(low), b_low)
        state[span, :] = jnp.exp(jnp.where(upper, end0, end1)) * s_pair + fresh


def bwd_kernel(
    x_ref, bc_ref, dt_ref, cum_ref, cumt_ref, skip_ref, dy_ref, start_ref, later_ref,
    feed_ref, before_ref, rim_ref, taps_ref, raw_ref, bias_ref, rate_ref, pick_ref,
    back_ref, first_ref, sums_ref, head_sums_ref,
    adjoint, dye, uw, xdu, dyi, udu, window, back,
):
    channels = feed_ref.shape[1]

    @pl.when(pl.program_id(0) == 0)
    def _():
        adjoint[...] = later_ref[...].astype(full)
        back[CHUNK:, :] = jnp.zeros((8, channels), full)
        sums_ref[...] = jnp.zeros_like(sums_ref)
        head_sums_ref[...] = jnp.zeros_like(head_sums_ref)

    at_start = pl.program_id(0) == pl.num_programs(0) - 1
    window[:RIM, :] = jnp.where(at_start, rim_ref[...].astype(full), before_ref[...].astype(full))
    window[RIM:, :] = feed_ref[...].astype(full)

    heads = cumt_ref.shape[0]
    inner = heads * HEADDIM
    b_low = bc_ref[:, :STATE].astype(low)
    c_low = bc_ref[:, STATE:].astype(low)
    row = lax.broadcasted_iota(jnp.int32, (CHUNK, CHUNK), 0)
    col = lax.broadcasted_iota(jnp.int32, (CHUNK, CHUNK), 1)
    left = col < HEADDIM
    causal = row >= col
    onward = (row <= col).astype(low)
    masked = jnp.where(causal, dot_nt(c_low, b_low), 0.0)
    d_affinity = jnp.zeros((CHUNK, CHUNK), full)
    dlog = jnp.zeros((CHUNK, LANES), full)
    for pair in range(heads // 2):
        h0, h1 = 2 * pair, 2 * pair + 1
        span = slice(pair * LANES, (pair + 1) * LANES)
        cum0 = jnp.broadcast_to(cum_ref[:, h0 : h0 + 1], (CHUNK, CHUNK))
        cum1 = jnp.broadcast_to(cum_ref[:, h1 : h1 + 1], (CHUNK, CHUNK))
        m0 = jnp.exp(jnp.minimum(cum0 - cumt_ref[h0 : h0 + 1, :], 0.0))
        m1 = jnp.exp(jnp.minimum(cum1 - cumt_ref[h1 : h1 + 1, :], 0.0))
        w0 = m0 * masked
        w1 = m1 * masked
        dt_pair = jnp.where(left, dt_ref[:, h0 : h0 + 1], dt_ref[:, h1 : h1 + 1])
        x_pair = x_ref[:, span]
        u = x_pair * dt_pair
        u_low = u.astype(low)
        dy_pair = dy_ref[:, span]
        dy_low = dy_pair.astype(low)
        zero = jnp.zeros_like(dy_low)
        dy_both = jnp.concatenate([jnp.where(left, dy_low, zero), jnp.where(left, zero, dy_low)], axis=0)
        dw = dot_nt(dy_both, u_low)
        dw0, dw1 = dw[:CHUNK], dw[CHUNK:]
        d_affinity = d_affinity + dw0 * m0 + dw1 * m1
        z_both = jnp.concatenate([(dw0 * w0).astype(low), (dw1 * w1).astype(low)], axis=1)
        reach = dot_nn(onward, z_both)
        k0 = jnp.sum(jnp.where(row > col, reach[:, :CHUNK], 0.0), axis=1, keepdims=True)
        k1 = jnp.sum(jnp.where(row > col, reach[:, CHUNK:], 0.0), axis=1, keepdims=True)
        dlog = jnp.where(col == h0, k0, jnp.where(col == h1, k1, dlog))
        w_both = jnp.concatenate([w0.astype(low), w1.astype(low)], axis=0)
        cum_pair = jnp.where(left, cum0, cum1)
        end0 = cum_ref[CHUNK - 1 : CHUNK, h0 : h0 + 1]
        end1 = cum_ref[CHUNK - 1 : CHUNK, h1 : h1 + 1]
        ahead = jnp.exp(jnp.where(left, end0, end1) - cum_pair)
        since = jnp.exp(cum_pair)
        du_state = ahead * dot_nt(b_low, adjoint[span, :].astype(low))
        du = dot_tn(w_both, dy_both) + du_state
        back[:CHUNK, span] = dt_pair * du + skip_ref[:, span] * dy_pair
        sums_ref[CONV + 1 : CONV + 2, span] += jnp.sum(x_pair * dy_pair, axis=0, keepdims=True)
        y_state = since * dot_nt(c_low, start_ref[0, span, :])
        xdu[:, span] = (x_pair * du).astype(low)
        dyi[:, span] = (dy_pair * y_state).astype(low)
        udu[:, span] = (u * du_state).astype(low)
        dye[:, span] = (dy_pair * since).astype(low)
        uw[:, span] = (u * ahead).astype(low)
    pick = pick_ref[...]
    ddt = dot_nn(xdu[...], pick)
    by_state = dot_nn(dyi[...], pick)
    by_later = dot_nn(udu[...], pick)
    adjoint_now = adjoint[...]
    start_now = start_ref[0]
    both = adjoint_now * start_now.astype(full)
    by_head = jnp.sum(both.reshape(heads, HEADDIM, STATE), axis=1)
    by_head = jnp.concatenate([by_head, jnp.zeros((LANES - heads, STATE), full)], axis=0)
    over = dot_nt(jnp.ones((8, STATE), full), by_head, highest)
    ends = jnp.exp(cum_ref[CHUNK - 1 : CHUNK, :])
    dlog = dlog + over[0:1] * ends
    dlog = dlog + dot_nn((row <= col).astype(full), by_state, highest)
    dlog = dlog + dot_nn((row > col).astype(full), by_later, highest)
    rate = rate_ref[...]
    step = (ddt + rate * dlog) * jax.nn.sigmoid(raw_ref[...] + bias_ref[...])
    back_ref[:, channels:] = step.astype(low)
    head_sums_ref[0:1, :] += jnp.sum(step, axis=0, keepdims=True)
    head_sums_ref[1:2, :] += jnp.sum(dlog * rate * dt_ref[...], axis=0, keepdims=True)
    d_aff = jnp.where(causal, d_affinity, 0.0).astype(low)
    back[:CHUNK, inner : inner + STATE] = dot_tn(d_aff, c_low) + dot_nn(uw[...], adjoint_now.astype(low))
    back[:CHUNK, inner + STATE :] = dot_nn(d_aff, b_low) + dot_nn(dye[...], start_now)
    fresh = dot_tn(dye[...], c_low)
    for pair in range(heads // 2):
        h0, h1 = 2 * pair, 2 * pair + 1
        span = slice(pair * LANES, (pair + 1) * LANES)
        shrink = jnp.where(row < HEADDIM, ends[:, h0 : h0 + 1], ends[:, h1 : h1 + 1])
        adjoint[span, :] = shrink * adjoint_now[span, :] + fresh[span, :]
    for group in range(channels // LANES):
        span = slice(group * LANES, (group + 1) * LANES)
        taken = [
            window[RIM - CONV + 1 + k : RIM - CONV + 1 + k + CHUNK, span] for k in range(CONV)
        ]
        pre = taps_ref[CONV : CONV + 1, span]
        for k in range(CONV):
            pre = pre + taps_ref[k : k + 1, span] * taken[k]
        sig = jax.nn.sigmoid(pre)
        back_pre = back[:CHUNK, span] * (sig * (1.0 + pre * (1.0 - sig)))
        back[:CHUNK, span] = back_pre
        for k in range(CONV):
            sums_ref[k : k + 1, span] += jnp.sum(back_pre * taken[k], axis=0, keepdims=True)
        sums_ref[CONV : CONV + 1, span] += jnp.sum(back_pre, axis=0, keepdims=True)
        total = taps_ref[CONV - 1 : CONV, span] * back_pre
        for k in range(CONV - 1):
            total = total + taps_ref[k : k + 1, span] * back[CONV - 1 - k : CONV - 1 - k + CHUNK, span]
        back_ref[:, span] = total.astype(low)
    back[CHUNK:, :] = back[:8, :]

    @pl.when(at_start)
    def _():
        first_ref[...] = back[:8, :]


def ssm_forward(act, dt, cum, cum_t, skip_row, entering):
    rows = act.shape[0]
    heads = cum_t.shape[0]
    inner = heads * HEADDIM
    blocks = rows // CHUNK
    return pl.pallas_call(
        fwd_kernel,
        grid=(blocks,),
        in_specs=[
            pl.BlockSpec((CHUNK, inner), lambda i: (i, 0)),
            pl.BlockSpec((CHUNK, 2 * STATE), lambda i: (i, inner // (2 * STATE))),
            pl.BlockSpec((CHUNK, LANES), lambda i: (i, 0)),
            pl.BlockSpec((CHUNK, LANES), lambda i: (i, 0)),
            pl.BlockSpec((heads, CHUNK), lambda i: (0, i)),
            pl.BlockSpec((1, inner), lambda i: (0, 0)),
            pl.BlockSpec((inner, STATE), lambda i: (0, 0)),
        ],
        out_specs=[
            pl.BlockSpec((CHUNK, inner), lambda i: (i, 0)),
            pl.BlockSpec((1, inner, STATE), lambda i: (i, 0, 0)),
        ],
        out_shape=[
            jax.ShapeDtypeStruct((rows, inner), full),
            jax.ShapeDtypeStruct((blocks, inner, STATE), low),
        ],
        scratch_shapes=[pltpu.VMEM((inner, STATE), full)],
        compiler_params=pltpu.CompilerParams(
            dimension_semantics=("arbitrary",), vmem_limit_bytes=40 * 1024 * 1024
        ),
        cost_estimate=pl.CostEstimate(
            flops=rows * inner * 2 * 4 * STATE,
            bytes_accessed=rows * inner * 10,
            transcendentals=rows * heads * CHUNK * 2,
        ),
        name="ssm_forward",
    )(act, act, dt, cum, cum_t, skip_row, entering)


def ssm_backward(act, dt, cum, cum_t, skip_row, dy, starts, later, feed, rim, taps, raw, bias, rate):
    rows, channels = feed.shape
    lane_row = pl.BlockSpec((1, LANES), lambda i: (0, 0))
    per_block = CHUNK // RIM
    channel = lax.broadcasted_iota(jnp.int32, (cum_t.shape[0] * HEADDIM, LANES), 0)
    pick = (channel // HEADDIM == lax.broadcasted_iota(jnp.int32, channel.shape, 1)).astype(low)
    heads = cum_t.shape[0]
    inner = heads * HEADDIM
    blocks = rows // CHUNK
    last = blocks - 1
    return pl.pallas_call(
        bwd_kernel,
        grid=(blocks,),
        in_specs=[
            pl.BlockSpec((CHUNK, inner), lambda i: (last - i, 0)),
            pl.BlockSpec((CHUNK, 2 * STATE), lambda i: (last - i, inner // (2 * STATE))),
            pl.BlockSpec((CHUNK, LANES), lambda i: (last - i, 0)),
            pl.BlockSpec((CHUNK, LANES), lambda i: (last - i, 0)),
            pl.BlockSpec((heads, CHUNK), lambda i: (0, last - i)),
            pl.BlockSpec((1, inner), lambda i: (0, 0)),
            pl.BlockSpec((CHUNK, inner), lambda i: (last - i, 0)),
            pl.BlockSpec((1, inner, STATE), lambda i: (last - i, 0, 0)),
            pl.BlockSpec((inner, STATE), lambda i: (0, 0)),
            pl.BlockSpec((CHUNK, channels), lambda i: (last - i, 0)),
            pl.BlockSpec((RIM, channels), lambda i: (jnp.maximum((last - i) * per_block - 1, 0), 0)),
            pl.BlockSpec((RIM, channels), lambda i: (0, 0)),
            pl.BlockSpec((8, channels), lambda i: (0, 0)),
            pl.BlockSpec((CHUNK, LANES), lambda i: (last - i, 0)),
            lane_row,
            lane_row,
            pl.BlockSpec((inner, LANES), lambda i: (0, 0)),
        ],
        out_specs=[
            pl.BlockSpec((CHUNK, channels + LANES), lambda i: (last - i, 0)),
            pl.BlockSpec((8, channels), lambda i: (0, 0)),
            pl.BlockSpec((8, channels), lambda i: (0, 0)),
            pl.BlockSpec((8, LANES), lambda i: (0, 0)),
        ],
        out_shape=[
            jax.ShapeDtypeStruct((rows, channels + LANES), low),
            jax.ShapeDtypeStruct((8, channels), full),
            jax.ShapeDtypeStruct((8, channels), full),
            jax.ShapeDtypeStruct((8, LANES), full),
        ],
        scratch_shapes=[
            pltpu.VMEM((inner, STATE), full),
            pltpu.VMEM((CHUNK, inner), low),
            pltpu.VMEM((CHUNK, inner), low),
            pltpu.VMEM((CHUNK, inner), low),
            pltpu.VMEM((CHUNK, inner), low),
            pltpu.VMEM((CHUNK, inner), low),
            pltpu.VMEM((CHUNK + RIM, channels), full),
            pltpu.VMEM((CHUNK + 8, channels), full),
        ],
        compiler_params=pltpu.CompilerParams(
            dimension_semantics=("arbitrary",), vmem_limit_bytes=40 * 1024 * 1024
        ),
        cost_estimate=pl.CostEstimate(
            flops=rows * inner * 2 * 16 * STATE,
            bytes_accessed=rows * inner * 16,
            transcendentals=rows * heads * CHUNK * 2,
        ),
        name="ssm_backward",
    )(act, act, dt, cum, cum_t, skip_row, dy, starts, later, feed, feed, rim, taps, raw, bias, rate, pick)


def heads_to_channels(values):
    heads = values.shape[1]
    head = lax.broadcasted_iota(jnp.int32, (heads, heads * HEADDIM), 0)
    channel = lax.broadcasted_iota(jnp.int32, (heads, heads * HEADDIM), 1)
    return dot_nn(values, (channel // HEADDIM == head).astype(full), highest)


def silu_slope(value, sig):
    return sig * (1.0 + value * (1.0 - sig))


def layer_forward(hidden, before, valid, weights, params):
    gain, taps, step_bias, decay_log, skip, out_gain = params
    feed_weight, gate_weight, out_weight = weights
    rows, width = hidden.shape
    heads = step_bias.shape[0]
    inner = heads * HEADDIM
    channels = inner + 2 * STATE
    norm = lax.rsqrt(jnp.mean(hidden * hidden, axis=-1, keepdims=True) + epsilon)
    normed = (hidden * norm * gain).astype(low)
    feed_all = dot_nn(normed, feed_weight)
    feed = feed_all[:, :channels].astype(low)
    raw = feed_all[:, channels:]
    before = before.astype(full)
    before_norm = lax.rsqrt(jnp.mean(before * before, axis=-1, keepdims=True) + epsilon)
    rim = dot_nn((before * before_norm * gain).astype(low), feed_weight[:, :channels]).astype(low)
    gate = dot_nn(normed, gate_weight)
    lanes = ((0, 0), (0, LANES - heads))
    bias = jnp.pad(step_bias[None], lanes)
    rate = jnp.pad(-jnp.exp(decay_log)[None], lanes)
    taps = jnp.pad(taps, ((0, 8 - CONV - 1), (0, 0)))
    act, dt, cum, cum_t, since, local_state = mixer_prep(feed, rim, taps, raw, bias, rate, heads)
    shrink = jnp.repeat(since[rows - 1, :heads], HEADDIM)[:, None]
    entering = chain(local_state, shrink, 1)
    skip_row = jnp.repeat(skip, HEADDIM)[None]
    scan = (act, dt, cum, cum_t, skip_row)
    conv = (feed, rim, taps, raw, bias, rate)
    ssm_out, starts = ssm_forward(*scan, entering)
    gated = ssm_out * (gate * jax.nn.sigmoid(gate))
    squares = jnp.sum(gated * gated, axis=-1)
    scaled = (gated * out_gain).astype(low)
    term = dot_nt(scaled, out_weight).astype(low)
    branch = term.astype(full) + swap_cores(term).astype(full)
    squares = squares + swap_cores(squares)
    out_norm = lax.rsqrt(squares / INNER + epsilon)[:, None]
    result = hidden + valid * out_norm * branch
    kept = (
        hidden, norm, normed, act, gate, since, shrink,
        scan, conv, starts, ssm_out, scaled, branch.astype(low), out_norm,
    )
    return result, kept


def chain(local_state, shrink, steps):
    entering = shifted(local_state.astype(low), "ctx", steps)
    for _ in range(lax.axis_size("ctx") - 2):
        leaving = shrink * entering.astype(full) + local_state
        entering = shifted(leaving.astype(low), "ctx", steps)
    return entering


def layer_backward(incoming, valid, weights, params, kept, pending=None):
    gain, taps, step_bias, decay_log, skip, out_gain = params
    feed_weight, gate_weight, out_weight = weights
    (
        hidden, norm, normed, act, gate, since, shrink,
        scan, conv, starts, ssm_out, scaled, branch, out_norm,
    ) = kept
    rows, width = hidden.shape
    heads = step_bias.shape[0]
    inner = heads * HEADDIM
    channels = inner + 2 * STATE
    back_branch = (valid * incoming).astype(low)
    back_normed = dot_nn(back_branch, out_weight)
    if pending is not None:
        pair, feed = pending
        back_normed, (pair.sums, feed.sums) = tied(back_normed, (pair.sums, feed.sums))
        pair.sums = pair_sum(pair.sums)
        feed.second()
    back_wide = back_branch.astype(full)
    grad_out = dot_tn((back_wide * out_norm).astype(low), scaled).astype(low)
    along = jnp.sum(back_wide * branch.astype(full), axis=-1, keepdims=True)
    sig = jax.nn.sigmoid(gate)
    silu = gate * sig
    gated = ssm_out * silu
    grad_out_gain = jnp.sum(back_normed * gated * out_norm, axis=0)
    back_gated = out_norm * out_gain * back_normed - gated * (out_norm**3 * along / INNER)
    back_ssm = back_gated * silu
    back_gate = (back_gated * ssm_out * silu_slope(gate, sig)).astype(low)
    grad_gate = dot_tn(normed, back_gate).astype(low)
    weighted = (back_ssm * heads_to_channels(since[:, :heads])).astype(low)
    local_adjoint = dot_tn(weighted, act[:, inner + STATE :].astype(low))
    later = chain(local_adjoint, shrink, -1)
    early = whole_reduction(grad_gate, grad_out)
    if pending is not None:
        back_ssm, feed.sums = tied(back_ssm, feed.sums)
        feed.sums = feed_sum(feed.sums, inner)
    early.first()
    back_all, first_rows, sums, head_sums = ssm_backward(*scan, back_ssm, starts, later, *conv)
    following = shifted(first_rows, "ctx", -1)
    taps = conv[2]
    edge = sum(
        jnp.pad(taps[k] * following[: CONV - 1 - k], ((RIM - CONV + 1 + k, 0), (0, LANES))) for k in range(CONV - 1)
    )
    back_all = lax.dynamic_update_slice_in_dim(
        back_all, (back_all[rows - RIM :].astype(full) + edge).astype(low), rows - RIM, 0
    )
    back_all, early.sums = tied(back_all, early.sums)
    if pending is not None:
        back_all, (pair.sums, feed.sums) = tied(back_all, (pair.sums, feed.sums))
    early.second()
    grad_skip = jnp.sum(sums[CONV + 1, :inner].reshape(heads, HEADDIM), axis=1)
    grad_step_bias, grad_decay = head_sums[0, :heads], head_sums[1, :heads]
    grad_taps = sums[: CONV + 1]
    term = (dot_nt(back_all, feed_weight) + dot_nt(back_gate, gate_weight)).astype(low)
    back_in = term.astype(full) + swap_cores(term).astype(full)
    grad_feed = dot_tn(normed, back_all).astype(low)
    grad_gain = jnp.sum(back_in * hidden * norm, axis=0)
    scaled_in = back_in * gain
    along_in = jnp.sum(scaled_in * hidden, axis=-1, keepdims=True)
    delta = norm * scaled_in - hidden * (norm**3 * along_in / width)
    small = jnp.concatenate(
        [
            grad_taps[:, :inner].reshape(-1), grad_taps[:, inner:].reshape(-1),
            grad_out_gain, grad_step_bias, grad_decay, grad_skip, grad_gain,
        ]
    )
    return delta, grad_feed, small, early


class Reduction:
    def __init__(self, half_a, half_b):
        self.half_a, self.half_b = half_a, half_b

    def first(self):
        ndp, nctx = lax.axis_size("dp"), lax.axis_size("ctx")

        def rows_of(half, owners):
            array, low_row, high_row = half
            each = array.shape[0] // (ndp * nctx)
            return jnp.concatenate(
                [
                    lax.dynamic_slice_in_dim(array, owner * each + low_row, high_row - low_row, 0)
                    for owner in owners
                ],
                axis=0,
            )

        self.sums = (
            scatter_sum(
                lambda at: rows_of(self.half_a, [i * nctx + at for i in range(ndp)]), "ctx"
            ).astype(low),
            scatter_sum(
                lambda at: rows_of(self.half_b, [at * nctx + j for j in range(nctx)]), "dp"
            ).astype(low),
        )

    def second(self):
        def own(value, axis):
            each = value.shape[0] // lax.axis_size(axis)
            return scatter_sum(
                lambda at: lax.dynamic_slice_in_dim(value, at * each, each, 0), axis
            ).astype(low)

        self.sums = own(self.sums[0], "dp"), own(self.sums[1], "ctx")


def whole_reduction(first, second):
    rows = first.shape[0] // (lax.axis_size("dp") * lax.axis_size("ctx"))
    return Reduction((first, 0, rows), (second, 0, rows))


def split_reduction(array):
    rows = array.shape[0] // (lax.axis_size("dp") * lax.axis_size("ctx"))
    return Reduction((array, 0, rows // 2), (array, rows // 2, rows))


def lanes_of(value, at, inner):
    each = inner // lax.axis_size("tp")
    return lax.dynamic_slice_in_dim(value, at * each, each, 1)


def pair_sum(sums):
    return scatter_sum(lambda at: columns(lanes_of(part, at, part.shape[1]) for part in sums), "tp")


def feed_sum(sums, inner, small=None):
    joined = jnp.concatenate(sums, axis=0)

    def pick(at):
        block = columns([lanes_of(joined, at, inner), joined[:, inner:]])
        if small is not None:
            block = jnp.concatenate([block, as_rows(small, block.shape[1])], axis=0)
        return block

    return scatter_sum(pick, "tp")


def on_device(
    acts,
    cotangent,
    lengths,
    norm_gain,
    proj_gate_x,
    proj_state,
    proj_step,
    conv_inner,
    conv_state,
    step_bias,
    decay_log,
    skip_weight,
    out_gain,
    proj_out,
):
    micro_count, rows, width = (acts.shape[0], acts.shape[2], acts.shape[3])
    tp_count = lax.axis_size("tp")
    core = lax.axis_index("section")
    lane = lax.axis_index("tp")
    first = core == 0
    own_rows = proj_gate_x.shape[1]
    half = proj_gate_x.shape[3] // 2
    step_half = proj_step.shape[2] // 2
    heads = step_half * tp_count
    inner = half * tp_count
    quarter = 2 * STATE // tp_count
    wide = quarter

    state_part = lax.dynamic_slice_in_dim(proj_state[0], lane * quarter, quarter, 1)

    def pack(c):
        step = proj_step[0, :, c * step_half : (c + 1) * step_half]
        tail = jnp.pad(columns([step, norm_gain[0][:, None]]), ((0, 0), (0, wide - step_half - 1)))
        return columns(
            [
                proj_gate_x[0, :, 1, c * half : (c + 1) * half],
                state_part,
                tail,
                proj_gate_x[0, :, 0, c * half : (c + 1) * half],
                proj_out[0, c * half : (c + 1) * half].T,
            ]
        )

    def pack_small(c):
        vector = jnp.concatenate(
            [
                conv_inner[0, :, c * half : (c + 1) * half].reshape(-1),
                out_gain[0, c * half : (c + 1) * half],
                step_bias[0, c * step_half : (c + 1) * step_half],
                decay_log[0, c * step_half : (c + 1) * step_half],
                skip_weight[0, c * step_half : (c + 1) * step_half],
                conv_state[0].reshape(-1),
            ]
        )
        parts = []
        for _ in range(3):
            part = lax.reduce_precision(vector, 8, 7)
            parts.append(part.astype(low))
            vector = vector - part
        return as_rows(jnp.concatenate(parts), cut)

    def both_layers(make):
        zero, one = make(0), make(1)
        keep = jnp.where(first, zero, one)
        came = swap_cores(jnp.where(first, one, zero))
        return jnp.where(first, keep, came), jnp.where(first, came, keep)

    def layer_params(rows_of_small):
        size = (CONV + 1) * half + half + 3 * step_half + (CONV + 1) * 2 * STATE
        three = rows_of_small.reshape(tp_count, -1)[:, : 3 * size].reshape(tp_count, 3, size)
        part = jnp.sum(three.astype(full), axis=1)
        at = (CONV + 1) * half
        taps_inner = jnp.moveaxis(part[:, :at].reshape(tp_count, CONV + 1, half), 0, 1)
        gains = part[:, at : at + half].reshape(-1)
        at += half
        scalars = []
        for _ in range(3):
            scalars.append(part[:, at : at + step_half].reshape(-1))
            at += step_half
        taps_state = part[0, at:].reshape(CONV + 1, 2 * STATE)
        taps = columns([taps_inner.reshape(CONV + 1, inner), taps_state])
        return taps, scalars[0], scalars[1], scalars[2], gains

    cut = half + quarter + wide
    middle = tp_count // 2

    def gather_item(part, sections):
        def side(pieces):
            parts, at = [], 0
            for size in sections:
                parts.append(columns(pieces[..., at : at + size]))
                at += size
            return columns(parts)

        half_a, half_b = gather_rows(side(part[:middle]), side(part[middle:]))
        result, at = [], 0
        for size in sections:
            result.append((half_a[:, at : at + middle * size], half_b[:, at : at + middle * size]))
            at += middle * size
        return result

    def feed_weights(parts):
        tails = [side.reshape(-1, middle, wide)[:, :, :step_half].reshape(-1, heads // 2) for side in parts[2]]
        gain = parts[2][0][:, step_half].astype(full)
        steps = jnp.pad(columns(tails), ((0, 0), (0, LANES - heads)))
        return columns(parts[0] + parts[1] + (steps,)), gain

    own_acts = lax.dynamic_index_in_dim(acts[:, 0], lane, 0, False)
    before = shifted(own_acts[rows - RIM :], "ctx", 1)
    smalls = both_layers(pack_small)
    packs = both_layers(pack)
    feed_sections, pair_sections = (half, quarter, wide), (half, half)
    along_feed = ring_gather(jnp.concatenate([packs[0][:, :cut], smalls[0]], axis=0), "tp")
    pair_pack, along_feed = tied(packs[0][:, cut:], along_feed)
    along_pair = ring_gather(pair_pack, "tp")
    feed_parts = gather_item(along_feed[:, :own_rows], feed_sections)
    last_pack, along_pair = tied(packs[1], along_pair)
    small_pad = jnp.pad(smalls[1], ((0, 0), (0, last_pack.shape[1] - cut)))
    along_last = ring_gather(jnp.concatenate([last_pack, small_pad], axis=0), "tp")
    pair_parts = gather_item(along_pair, pair_sections)
    along_last, pair_parts = tied(along_last, pair_parts)
    last_parts = gather_item(along_last[:, :own_rows, :cut], feed_sections)
    along_last, last_parts = tied(along_last, last_parts)
    last_parts += gather_item(along_last[:, :own_rows, cut:], pair_sections)
    feed_first, gain_first = feed_weights(feed_parts)
    feed_last, gain_last = feed_weights(last_parts[:3])
    weights = [
        (feed_first, columns(pair_parts[0]), columns(pair_parts[1])),
        (feed_last, columns(last_parts[3]), columns(last_parts[4])),
    ]
    params = [
        (gain_first,) + layer_params(along_feed[:, own_rows:]),
        (gain_last,) + layer_params(along_last[:, own_rows:, :cut]),
    ]

    places = lax.axis_index("ctx") * rows + jnp.arange(rows, dtype=jnp.int32)
    length = lax.dynamic_index_in_dim(lengths[:, 0], lane, 0, False)
    valid = (places < length).astype(full)[:, None]
    hidden = own_acts.astype(full)
    out_grad = lax.dynamic_index_in_dim(cotangent[:, 0], lane, 0, False)

    result_first, kept_first = layer_forward(hidden, before, valid, weights[0], params[0])
    low_first = result_first.astype(low)
    before = shifted(low_first[rows - RIM :], "ctx", 1)
    result_last, kept_last = layer_forward(low_first.astype(full), before, valid, weights[1], params[1])
    own_result = jnp.where(first, low_first, result_last.astype(low))
    quarter_rows = rows // tp_count
    section_out = spread_rows(own_result.reshape(tp_count, quarter_rows, width), (0, 1))

    delta_last, feed_last, small_last, pair_last = layer_backward(
        out_grad, valid, weights[1], params[1], kept_last
    )
    last = split_reduction(feed_last)
    last.first()
    spread_last = spread_rows(delta_last.astype(low).reshape(tp_count, quarter_rows, width), (1,))
    incoming = (out_grad + delta_last).astype(low).astype(full)
    delta_first, feed_first, small_first, pair_first = layer_backward(
        incoming, valid, weights[0], params[0], kept_first, (pair_last, last)
    )
    grad_first = (incoming + delta_first).astype(low)
    feed_first, (grad_first, pair_first.sums) = tied(feed_first, (grad_first, pair_first.sums))
    feed = split_reduction(feed_first)
    feed.first()
    pair_first_sum = pair_sum(pair_first.sums)
    small = jnp.stack([small_first, small_last])
    spread_first = spread_rows(grad_first.reshape(tp_count, quarter_rows, width), (0,))
    small = all_sum(all_sum(small, "ctx"), "dp")
    feed.second()
    feed_sums = feed_sum(feed.sums, inner, small.astype(low).reshape(-1))
    own_cotangent = lax.dynamic_slice_in_dim(
        cotangent[:, 0], lane * quarter_rows, quarter_rows, 1
    )
    input_grad = jnp.where(
        first, spread_first.astype(full), own_cotangent + spread_last.astype(full)
    )

    pair_keep = jnp.where(first, pair_first_sum, pair_last.sums)
    pair_came = swap_cores(jnp.where(first, pair_last.sums, pair_first_sum))
    size = small_first.shape[0]
    small_sums = feed_sums[own_rows:].reshape(-1)[: 2 * size].reshape(2, size)
    sums_last = last.sums
    total_width = sums_last.shape[1]
    joined = [
        jnp.concatenate([sums, as_rows(vector, total_width)])
        for sums, vector in zip((feed_sums[:own_rows], sums_last), small_sums)
    ]
    keep = jnp.where(first, joined[0], joined[1])
    came = swap_cores(jnp.where(first, joined[1], joined[0]))
    small_keep = keep[own_rows:].reshape(-1)[:size]
    small_came = came[own_rows:].reshape(-1)[:size]
    keep, came = keep[:own_rows], came[:own_rows]

    def halves(kept_part, came_part, axis):
        zero = jnp.where(first, kept_part, came_part)
        one = jnp.where(first, came_part, kept_part)
        return jnp.concatenate([zero, one], axis=axis)

    def own_lane(value, shape, axis):
        return lax.dynamic_index_in_dim(value.reshape(shape), lane, axis, False)

    grad_gate = halves(pair_keep[:, :half], pair_came[:, :half], 1)
    grad_out = halves(pair_keep[:, half:].T, pair_came[:, half:].T, 0)
    at = 0
    grad_x = halves(keep[:, at : at + half], came[:, at : at + half], 1)
    at += half
    grad_state = keep[:, at : at + 2 * STATE] + came[:, at : at + 2 * STATE]
    at += 2 * STATE + lane * step_half
    grad_step = halves(
        lax.dynamic_slice_in_dim(keep, at, step_half, 1), lax.dynamic_slice_in_dim(came, at, step_half, 1), 1
    )
    grad_gate_x = jnp.stack([grad_gate, grad_x], axis=1)

    at = (CONV + 1) * inner
    taps_shape = (CONV + 1, tp_count, half)
    grad_conv_inner = halves(
        own_lane(small_keep[:at], taps_shape, 1), own_lane(small_came[:at], taps_shape, 1), 1
    )
    end = at + (CONV + 1) * 2 * STATE
    grad_conv_state = (small_keep[at:end] + small_came[at:end]).reshape(CONV + 1, 2 * STATE)
    at = end
    vectors = []
    for size in (inner, heads, heads, heads):
        shape = (tp_count, size // tp_count)
        vectors.append(
            halves(
                own_lane(small_keep[at : at + size], shape, 0),
                own_lane(small_came[at : at + size], shape, 0),
                0,
            )
        )
        at += size
    owner = lax.axis_index("dp") * lax.axis_size("ctx") + lax.axis_index("ctx")
    grad_norm_gain = lax.dynamic_slice_in_dim(small_keep[at:], owner * own_rows, own_rows, 0)
    return (
        section_out[None, :, None],
        input_grad[None, :, None],
        grad_norm_gain[None],
        grad_gate_x[None],
        grad_state[None],
        grad_step[None],
        grad_conv_inner[None],
        grad_conv_state[None],
        vectors[1][None],
        vectors[2][None],
        vectors[3][None],
        vectors[0][None],
        grad_out[None],
    )


def solution(mesh):
    placed = (
        P(None, "dp", "ctx", None),
        P(None, "dp", "ctx", None),
        P(None, "dp"),
        P("section", ("dp", "ctx")),
        P("section", ("dp", "ctx"), None, "tp"),
        P("section", ("dp", "ctx"), None),
        P("section", ("dp", "ctx"), "tp"),
        P("section", None, "tp"),
        P("section", None, None),
        P("section", "tp"),
        P("section", "tp"),
        P("section", "tp"),
        P("section", "tp"),
        P("section", "tp", ("dp", "ctx")),
    )
    return jax.shard_map(
        on_device,
        mesh=mesh,
        in_specs=placed,
        out_specs=(
            P("section", None, "dp", ("ctx", "tp"), None),
            P("section", None, "dp", ("ctx", "tp"), None),
            P("section", ("dp", "ctx")),
            P("section", ("dp", "ctx"), None, "tp"),
            P("section", ("dp", "ctx"), None),
            P("section", ("dp", "ctx"), "tp"),
            P("section", None, "tp"),
            P("section", None, None),
            P("section", "tp"),
            P("section", "tp"),
            P("section", "tp"),
            P("section", "tp"),
            P("section", "tp", ("dp", "ctx")),
        ),
        check_vma=False,
    )
```

profile of v0, /device:TPU:1, one launch (start us, length us, event | category | flops | bytes accessed | tf_op | source)
XLA Modules:
  0.0 772.8 jit_solution(10360644336246744708)
XLA Ops:
  25.2 13.9 %collective-permute-done.3 = bf16[288,384]{1,0:T(8,128)(2,1)S(1)} collective-permute-done((bf16[288,384]{1,0:T(8,128)(2,1)S(1)}, bf16[288,384]{1,0:T(8,128)(2,1)S(1)}, u32[]{:S(2)}, u32[]{:S(2)}) %collective-permute-start.3) | collective-permute-done | bytes 221216 | tf_op jit(solution)/shard_map/ppermute | solution.py:50
  47.6 17.2 %collective-permute-done.12 = bf16[256,512]{1,0:T(8,128)(2,1)S(1)} collective-permute-done((bf16[256,512]{1,0:T(8,128)(2,1)S(1)}, bf16[256,512]{1,0:T(8,128)(2,1)S(1)}, u32[]{:S(2)}, u32[]{:S(2)}) %collective-permute-start.12) | collective-permute-done | bytes 262176 | tf_op jit(solution)/shard_map/ppermute | solution.py:50
  69.4 7.2 collective-permute-done.14
  76.7 34.0 %collective-permute-done.15 = bf16[288,896]{1,0:T(8,128)(2,1)S(1)} collective-permute-done((bf16[288,896]{1,0:T(8,128)(2,1)S(1)}, bf16[288,896]{1,0:T(8,128)(2,1)S(1)}, u32[]{:S(2)}, u32[]{:S(2)}) %collective-permute-start.15) | collective-permute-done | bytes 516128 | tf_op jit(solution)/shard_map/ppermute | solution.py:50
  117.6 11.2 %collective-permute-done.6 = bf16[2,256,768]{2,1,0:T(8,128)(2,1)S(1)} collective-permute-done((bf16[2,256,768]{2,1,0:T(8,128)(2,1)S(1)}, bf16[2,256,768]{2,1,0:T(8,128)(2,1)S(1)}, u32[]{:S(2)}, u32[]{:S(2)}) %collective-permute-start.6) | collective-permute-done | bytes 786464 | tf_op jit(solution)/shard_map/ppermute | solution.py:50
  134.9 5.9 fusion.167
  142.8 9.7 %mixer_prep.2 = (f32[1024,1280]{1,0:T(8,128)S(1)}, f32[1024,128]{1,0:T(8,128)S(1)}, f32[1024,128]{1,0:T(8,128)S(1)}, f32[16,1024]{1,0:T(8,128)S(1)}, f32[1024,128]{1,0:T(8,128)S(1)}, /*index=5*/f32[1024,128]{1,0:T(8,128)S(1)}) custom-call(bf16[1024,1280]{1,0:T(8,128)(2,1)S(1)} %slice.929.feed_ref.before_ref, bf16[16,1280]{1,0:T(8,128)(2,1)S(1)} %fusion.52.rim_ref, ...), custom_call_target="tpu_custom_call" | custom-call | flops 268435456 | bytes 7864320 | tf_op jit(solution)/shard_map/mixer_prep/pallas_call | solution.py:195
  158.2 12.6 %ssm_forward.2 = (f32[1024,1024]{1,0:T(8,128)S(1)}, bf16[8,1024,128]{2,1,0:T(8,128)(2,1)S(1)}) custom-call(f32[1024,1280]{1,0:T(8,128)S(1)} %get-tuple-element.75.x_ref.bc_ref, f32[1024,1280]{1,0:T(8,128)S(1)} %get-tuple-element.75.x_ref.bc_ref, f32[1024,128]{1,0:T(8,128)S(1)} %get-tuple-element.76.dt_ref, f32[1024,128]{1,0:T(8,128)S(1)} %get-tuple-element.77.cum_ref, ...), custom_call_target="tpu_custom_call" | custom-call | flops 1073741824 | bytes 10485760 | tf_op jit(solution)/shard_map/ssm_forward/pallas_call | solution.py:401
  190.7 8.3 %multiply_reduce_fusion.3 = (f32[1024]{0:T(1024)S(1)}, f32[1024,1024]{1,0:T(8,128)S(1)}, f32[1024,1024]{1,0:T(8,128)}) fusion(f32[1024,1024]{1,0:T(8,128)} %copy-done.10, bf16[1024,1024]{1,0:T(8,128)(2,1)} %constant_dynamic-update-slice_fusion.4, f32[1024]{0:T(1024)S(1)} %convert_reduce_fusion.1, f32[1024]{0:T(1024)S(1)} %add_rsqrt_fusion.3, ...), kind=kOutput, calls=%fused_computation.68 | convolution fusion | flops 2159016960 | bytes 16789508 | tf_op jit(solution)/shard_map/dot_general | solution.py:25
  206.8 5.6 collective-permute-start.22
  218.5 12.8 %collective-permute-done.26 = bf16[2,256,768]{2,1,0:T(8,128)(2,1)S(1)} collective-permute-done((bf16[2,256,768]{2,1,0:T(8,128)(2,1)S(1)}, bf16[2,256,768]{2,1,0:T(8,128)(2,1)S(1)}, u32[]{:S(2)}, u32[]{:S(2)}) %collective-permute-start.26) | collective-permute-done | bytes 786464 | tf_op jit(solution)/shard_map/ppermute | solution.py:50
  262.3 8.8 %collective-permute-done.27 = bf16[16,1024]{1,0:T(8,128)(2,1)S(1)} collective-permute-done((bf16[16,1024]{1,0:T(8,128)(2,1)S(1)}, bf16[16,1024]{1,0:T(8,128)(2,1)S(1)}, u32[]{:S(2)}, u32[]{:S(2)}) %collective-permute-start.27) | collective-permute-done | bytes 32800 | tf_op jit(solution)/shard_map/ppermute | solution.py:45
  271.7 9.7 %mixer_prep.3 = (f32[1024,1280]{1,0:T(8,128)S(1)}, f32[1024,128]{1,0:T(8,128)S(1)}, f32[1024,128]{1,0:T(8,128)S(1)}, f32[16,1024]{1,0:T(8,128)S(1)}, f32[1024,128]{1,0:T(8,128)S(1)}, /*index=5*/f32[1024,128]{1,0:T(8,128)S(1)}) custom-call(bf16[1024,1280]{1,0:T(8,128)(2,1)S(1)} %slice.928.feed_ref.before_ref, bf16[16,1280]{1,0:T(8,128)(2,1)S(1)} %fusion.49.rim_ref, ...), custom_call_target="tpu_custom_call" | custom-call | flops 268435456 | bytes 7864320 | tf_op jit(solution)/shard_map/mixer_prep/pallas_call | solution.py:195
  289.7 12.2 %ssm_forward.3 = (f32[1024,1024]{1,0:T(8,128)S(1)}, bf16[8,1024,128]{2,1,0:T(8,128)(2,1)S(1)}) custom-call(f32[1024,1280]{1,0:T(8,128)S(1)} %get-tuple-element.96.x_ref.bc_ref, f32[1024,1280]{1,0:T(8,128)S(1)} %get-tuple-element.96.x_ref.bc_ref, f32[1024,128]{1,0:T(8,128)S(1)} %get-tuple-element.97.dt_ref, f32[1024,128]{1,0:T(8,128)S(1)} %get-tuple-element.98.cum_ref, ...), custom_call_target="tpu_custom_call" | custom-call | flops 1073741824 | bytes 10485760 | tf_op jit(solution)/shard_map/ssm_forward/pallas_call | solution.py:401
  303.6 5.7 collective-permute-done.30
  333.8 7.2 fusion.60
  372.4 34.4 %ssm_backward.2 = (bf16[1024,1408]{1,0:T(8,128)(2,1)S(1)}, f32[8,1280]{1,0:T(8,128)}, f32[8,1280]{1,0:T(8,128)S(1)}, f32[8,128]{1,0:T(8,128)S(1)}) custom-call(f32[1024,1280]{1,0:T(8,128)} %copy-done.3, f32[1024,1280]{1,0:T(8,128)} %copy-done.3, f32[1024,128]{1,0:T(8,128)S(1)} %copy-done.21, f32[1024,128]{1,0:T(8,128)S(1)} %copy-done.23, ...), custom_call_target="tpu_custom_call" | custom-call | flops 4294967296 | bytes 16777216 | tf_op jit(solution)/shard_map/ssm_backward/pallas_call | solution.py:444
  424.6 10.8 %collective-permute-done.41 = bf16[512,1024]{1,0:T(8,128)(2,1)S(1)} collective-permute-done((bf16[512,1024]{1,0:T(8,128)(2,1)}, bf16[512,1024]{1,0:T(8,128)(2,1)S(1)}, u32[]{:S(2)}, u32[]{:S(2)}) %collective-permute-start.41) | collective-permute-done | bytes 1048608 | tf_op jit(solution)/shard_map/ppermute | solution.py:50
  451.3 10.0 %collective-permute-done.43 = bf16[256,1024]{1,0:T(8,128)(2,1)S(1)} collective-permute-done((bf16[256,1024]{1,0:T(8,128)(2,1)S(1)}, bf16[256,1024]{1,0:T(8,128)(2,1)S(1)}, u32[]{:S(2)}, u32[]{:S(2)}) %collective-permute-start.43) | collective-permute-done | bytes 524320 | tf_op jit(solution)/shard_map/ppermute | solution.py:50
  462.5 15.2 %collective-permute-done.45 = bf16[256,1408]{1,0:T(8,128)(2,1)S(1)} collective-permute-done((bf16[256,1408]{1,0:T(8,128)(2,1)S(1)}, bf16[256,1408]{1,0:T(8,128)(2,1)S(1)}, u32[]{:S(2)}, u32[]{:S(2)}) %collective-permute-start.45) | collective-permute-done | bytes 720928 | tf_op jit(solution)/shard_map/ppermute | solution.py:50
  480.0 5.2 fusion.4
  522.3 11.6 %collective-permute-done.54 = bf16[256,512]{1,0:T(8,128)(2,1)} collective-permute-done((bf16[256,512]{1,0:T(8,128)(2,1)}, bf16[256,512]{1,0:T(8,128)(2,1)}, u32[]{:S(2)}, u32[]{:S(2)}) %collective-permute-start.54) | collective-permute-done | bytes 262176 | tf_op jit(solution)/shard_map/ppermute | solution.py:50
  540.0 34.2 %ssm_backward.3 = (bf16[1024,1408]{1,0:T(8,128)(2,1)S(1)}, f32[8,1280]{1,0:T(8,128)S(1)}, f32[8,1280]{1,0:T(8,128)S(1)}, f32[8,128]{1,0:T(8,128)S(1)}) custom-call(f32[1024,1280]{1,0:T(8,128)} %copy-done.2, f32[1024,1280]{1,0:T(8,128)} %copy-done.2, f32[1024,128]{1,0:T(8,128)S(1)} %copy-done.17, f32[1024,128]{1,0:T(8,128)S(1)} %copy-done.19, ...), custom_call_target="tpu_custom_call" | custom-call | flops 4294967296 | bytes 16777216 | tf_op jit(solution)/shard_map/ssm_backward/pallas_call | solution.py:444
  581.4 11.4 %collective-permute-done.58 = bf16[256,640]{1,0:T(8,128)(2,1)} collective-permute-done((bf16[256,640]{1,0:T(8,128)(2,1)}, bf16[256,640]{1,0:T(8,128)(2,1)}, u32[]{:S(2)}, u32[]{:S(2)}) %collective-permute-start.58) | collective-permute-done | bytes 327712 | tf_op jit(solution)/shard_map/ppermute | solution.py:50
  592.8 23.8 %collective-permute-start.65 = (bf16[256,1024]{1,0:T(8,128)(2,1)}, bf16[256,1024]{1,0:T(8,128)(2,1)S(1)}, u32[]{:S(2)}, u32[]{:S(2)}) collective-permute-start(bf16[256,1024]{1,0:T(8,128)(2,1)} %get-tuple-element.248), channel_id=1, source_target_pairs={{16,17},{17,18},{18,19},{19,16},{20,21},{21,22},{22,23},{23,20},{2... | collective-permute-start | bytes 1572872 | tf_op jit(solution)/shard_map/ppermute | solution.py:114
  642.3 5.9 collective-permute-done.60
  674.5 22.2 %collective-permute-done.78 = bf16[256,512]{1,0:T(8,128)(2,1)} collective-permute-done((bf16[256,512]{1,0:T(8,128)(2,1)}, bf16[256,512]{1,0:T(8,128)(2,1)}, u32[]{:S(2)}, u32[]{:S(2)}) %collective-permute-start.78) | collective-permute-done | bytes 262176 | tf_op jit(solution)/shard_map/ppermute | solution.py:50
  701.8 6.7 collective-permute-start.80
  711.8 8.7 %collective-permute-done.69 = bf16[128,1408]{1,0:T(8,128)(2,1)S(1)} collective-permute-done((bf16[128,1408]{1,0:T(8,128)(2,1)S(1)}, bf16[128,1408]{1,0:T(8,128)(2,1)S(1)}, u32[]{:S(2)}, u32[]{:S(2)}) %collective-permute-start.69) | collective-permute-done | bytes 360480 | tf_op jit(solution)/shard_map/ppermute | solution.py:50
  725.7 5.4 fusion.23
  731.2 20.1 %collective-permute-done.75 = bf16[288,640]{1,0:T(8,128)(2,1)S(1)} collective-permute-done((bf16[288,640]{1,0:T(8,128)(2,1)S(1)}, bf16[288,640]{1,0:T(8,128)(2,1)S(1)}, u32[]{:S(2)}, u32[]{:S(2)}) %collective-permute-start.75) | collective-permute-done | bytes 368672 | tf_op jit(solution)/shard_map/ppermute | solution.py:50
  752.7 6.0 collective-permute-start.81
  (914 shorter events, 354.1 us)
Async XLA Ops:
  39.6 25.3 %collective-permute-start.12 = (bf16[256,512]{1,0:T(8,128)(2,1)S(1)}, bf16[256,512]{1,0:T(8,128)(2,1)S(1)}, u32[]{:S(2)}, u32[]{:S(2)}) collective-permute-start(bf16[256,512]{1,0:T(8,128)(2,1)S(1)} %slice.696), channel_id=1, source_target_pairs={{0,2},{1,3},{2,0},{3,1},{4,6},{5,7},{6,4},{7,5},{8,10},{9,11},{10,... | collective-permute-start | bytes 786440 | tf_op jit(solution)/shard_map/ppermute | solution.py:50
  65.3 45.5 %collective-permute-start.15 = (bf16[288,896]{1,0:T(8,128)(2,1)S(1)}, bf16[288,896]{1,0:T(8,128)(2,1)S(1)}, u32[]{:S(2)}, u32[]{:S(2)}) collective-permute-start(bf16[288,896]{1,0:T(8,128)(2,1)S(1)} %fusion.80), channel_id=1, source_target_pairs={{0,2},{1,3},{2,0},{3,1},{4,6},{5,7},{6,4},{7,5},{8,10},{9,11},{10,... | collective-permute-start | bytes 1548296 | tf_op jit(solution)/shard_map/ppermute | solution.py:50
  66.0 46.1 %collective-permute-start.16 = (bf16[288,896]{1,0:T(8,128)(2,1)S(1)}, bf16[288,896]{1,0:T(8,128)(2,1)S(1)}, u32[]{:S(2)}, u32[]{:S(2)}) collective-permute-start(bf16[288,896]{1,0:T(8,128)(2,1)S(1)} %fusion.80), channel_id=1, source_target_pairs={{0,1},{1,2},{2,3},{3,0},{4,5},{5,6},{6,7},{7,4},{8,9},{9,10},{10,1... | collective-permute-start | bytes 1548296 | tf_op jit(solution)/shard_map/ppermute | solution.py:50
  67.7 46.9 %collective-permute-start.17 = (bf16[256,1024]{1,0:T(8,128)(2,1)S(1)}, bf16[256,1024]{1,0:T(8,128)(2,1)S(1)}, u32[]{:S(2)}, u32[]{:S(2)}) collective-permute-start(bf16[256,1024]{1,0:T(8,128)(2,1)S(1)} %pad_maximum_fusion.35), channel_id=1, source_target_pairs={{0,4},{4,0},{1,5},{5,1},{2,6},{6,2},{3,7},{7,3},{8,12},{12,8},{9,1... | collective-permute-start | bytes 1572872 | tf_op jit(solution)/shard_map/ppermute | solution.py:50
  67.9 48.3 %collective-permute-start.19 = (bf16[256,1024]{1,0:T(8,128)(2,1)S(1)}, bf16[256,1024]{1,0:T(8,128)(2,1)S(1)}, u32[]{:S(2)}, u32[]{:S(2)}) collective-permute-start(bf16[256,1024]{1,0:T(8,128)(2,1)S(1)} %pad_maximum_fusion.36), channel_id=1, source_target_pairs={{0,8},{8,0},{1,9},{9,1},{2,10},{10,2},{3,11},{11,3},{4,12},{12,4},... | collective-permute-start | bytes 1572872 | tf_op jit(solution)/shard_map/ppermute | solution.py:50
  76.7 53.8 %collective-permute-start.8 = (bf16[2,256,768]{2,1,0:T(8,128)(2,1)S(1)}, bf16[2,256,768]{2,1,0:T(8,128)(2,1)S(1)}, u32[]{:S(2)}, u32[]{:S(2)}) collective-permute-start(bf16[2,256,768]{2,1,0:T(8,128)(2,1)S(1)} %pad_maximum_fusion.23), channel_id=1, source_target_pairs={{0,4},{4,0},{1,5},{5,1},{2,6},{6,2},{3,7},{7,3},{8,12},{12,8},{9,1... | collective-permute-start | bytes 2359304 | tf_op jit(solution)/shard_map/ppermute | solution.py:50
  116.0 55.7 %collective-permute-start.18 = (bf16[2,256,1024]{2,1,0:T(8,128)(2,1)}, bf16[2,256,1024]{2,1,0:T(8,128)(2,1)}, u32[]{:S(2)}, u32[]{:S(2)}) collective-permute-start(bf16[2,256,1024]{2,1,0:T(8,128)(2,1)} %pad_maximum_fusion.14), channel_id=1, source_target_pairs={{0,8},{8,0},{1,9},{9,1},{2,10},{10,2},{3,11},{11,3},{4,12},{12,4},... | collective-permute-start | bytes 3145736 | tf_op jit(solution)/shard_map/ppermute | solution.py:50
  117.6 56.9 %collective-permute-start.20 = (bf16[2,256,1024]{2,1,0:T(8,128)(2,1)}, bf16[2,256,1024]{2,1,0:T(8,128)(2,1)}, u32[]{:S(2)}, u32[]{:S(2)}) collective-permute-start(bf16[2,256,1024]{2,1,0:T(8,128)(2,1)} %pad_maximum_fusion.15), channel_id=1, source_target_pairs={{0,4},{4,0},{1,5},{5,1},{2,6},{6,2},{3,7},{7,3},{8,12},{12,8},{9,1... | collective-permute-start | bytes 3145736 | tf_op jit(solution)/shard_map/ppermute | solution.py:50
  187.2 25.3 %collective-permute-start.25 = (bf16[256,768]{1,0:T(8,128)(2,1)}, bf16[256,768]{1,0:T(8,128)(2,1)S(1)}, u32[]{:S(2)}, u32[]{:S(2)}) collective-permute-start(bf16[256,768]{1,0:T(8,128)(2,1)} %concatenate.264), channel_id=1, source_target_pairs={{0,8},{8,0},{1,9},{9,1},{2,10},{10,2},{3,11},{11,3},{4,12},{12,4},... | collective-permute-start | bytes 1179656 | tf_op jit(solution)/shard_map/ppermute | solution.py:50
  206.8 44.3 %collective-permute-start.22 = (bf16[1024,1024]{1,0:T(8,128)(2,1)}, bf16[1024,1024]{1,0:T(8,128)(2,1)}, u32[]{:S(2)}, u32[]{:S(2)}) collective-permute-start(bf16[1024,1024]{1,0:T(8,128)(2,1)} %convolution_convert_fusion.5), channel_id=1, source_target_pairs={{0,16},{16,0},{1,17},{17,1},{2,18},{18,2},{3,19},{19,3},{4,20},{20... | collective-permute-start | bytes 6291464 | tf_op jit(solution)/shard_map/ppermute | solution.py:98
  249.1 52.9 %collective-permute-start.32 = (bf16[2,256,1024]{2,1,0:T(8,128)(2,1)S(1)}, bf16[2,256,1024]{2,1,0:T(8,128)(2,1)S(1)}, u32[]{:S(2)}, u32[]{:S(2)}) collective-permute-start(bf16[2,256,1024]{2,1,0:T(8,128)(2,1)S(1)} %pad_maximum_fusion.17), channel_id=1, source_target_pairs={{0,4},{4,0},{1,5},{5,1},{2,6},{6,2},{3,7},{7,3},{8,12},{12,8},{9,1... | collective-permute-start | bytes 3145736 | tf_op jit(solution)/shard_map/ppermute | solution.py:50
  355.6 61.4 %collective-permute-start.35 = (bf16[256,1024]{1,0:T(8,128)(2,1)}, bf16[256,1024]{1,0:T(8,128)(2,1)}, u32[]{:S(2)}, u32[]{:S(2)}) collective-permute-start(bf16[256,1024]{1,0:T(8,128)(2,1)} %get-tuple-element.260), channel_id=1, source_target_pairs={{0,1},{1,2},{2,3},{3,0},{16,17},{17,18},{18,19},{19,16},{4,5},{5,6... | collective-permute-start | bytes 1572872 | tf_op jit(solution)/shard_map/ppermute | solution.py:114
  355.6 63.3 %collective-permute-start.36 = (bf16[256,1024]{1,0:T(8,128)(2,1)}, bf16[256,1024]{1,0:T(8,128)(2,1)}, u32[]{:S(2)}, u32[]{:S(2)}) collective-permute-start(bf16[256,1024]{1,0:T(8,128)(2,1)} %get-tuple-element.259), channel_id=1, source_target_pairs={{0,2},{1,3},{2,0},{3,1},{16,18},{17,19},{18,16},{19,17},{4,6},{5,7... | collective-permute-start | bytes 1572872 | tf_op jit(solution)/shard_map/ppermute | solution.py:114
  355.6 65.2 %collective-permute-start.37 = (bf16[256,1024]{1,0:T(8,128)(2,1)}, bf16[256,1024]{1,0:T(8,128)(2,1)}, u32[]{:S(2)}, u32[]{:S(2)}) collective-permute-start(bf16[256,1024]{1,0:T(8,128)(2,1)} %get-tuple-element.258), channel_id=1, source_target_pairs={{0,3},{1,0},{2,1},{3,2},{16,19},{17,16},{18,17},{19,18},{4,7},{5,4... | collective-permute-start | bytes 1572872 | tf_op jit(solution)/shard_map/ppermute | solution.py:114
  366.2 56.6 %collective-permute-start.40 = (bf16[512,1024]{1,0:T(8,128)(2,1)}, bf16[512,1024]{1,0:T(8,128)(2,1)}, u32[]{:S(2)}, u32[]{:S(2)}) collective-permute-start(bf16[512,1024]{1,0:T(8,128)(2,1)} %pad_maximum_fusion.18), channel_id=1, source_target_pairs={{0,4},{4,0},{1,5},{5,1},{2,6},{6,2},{3,7},{7,3},{8,12},{12,8},{9,1... | collective-permute-start | bytes 3145736 | tf_op jit(solution)/shard_map/ppermute | solution.py:50
  443.7 34.4 %collective-permute-start.42 = (bf16[1024,1024]{1,0:T(8,128)(2,1)S(1)}, bf16[1024,1024]{1,0:T(8,128)(2,1)S(1)}, u32[]{:S(2)}, u32[]{:S(2)}) collective-permute-start(bf16[1024,1024]{1,0:T(8,128)(2,1)S(1)} %add_convert_fusion.1), channel_id=1, source_target_pairs={{0,16},{16,0},{1,17},{17,1},{2,18},{18,2},{3,19},{19,3},{4,20},{20... | collective-permute-start | bytes 6291464 | tf_op jit(solution)/shard_map/ppermute | solution.py:98
  450.3 27.4 %collective-permute-start.45 = (bf16[256,1408]{1,0:T(8,128)(2,1)S(1)}, bf16[256,1408]{1,0:T(8,128)(2,1)S(1)}, u32[]{:S(2)}, u32[]{:S(2)}) collective-permute-start(bf16[256,1408]{1,0:T(8,128)(2,1)S(1)} %pad_maximum_fusion.30), channel_id=1, source_target_pairs={{0,4},{4,0},{1,5},{5,1},{2,6},{6,2},{3,7},{7,3},{8,12},{12,8},{9,1... | collective-permute-start | bytes 2162696 | tf_op jit(solution)/shard_map/ppermute | solution.py:50
  451.0 26.9 %collective-permute-start.46 = (bf16[256,1408]{1,0:T(8,128)(2,1)S(1)}, bf16[256,1408]{1,0:T(8,128)(2,1)S(1)}, u32[]{:S(2)}, u32[]{:S(2)}) collective-permute-start(bf16[256,1408]{1,0:T(8,128)(2,1)S(1)} %pad_maximum_fusion.31), channel_id=1, source_target_pairs={{0,8},{8,0},{1,9},{9,1},{2,10},{10,2},{3,11},{11,3},{4,12},{12,4},... | collective-permute-start | bytes 2162696 | tf_op jit(solution)/shard_map/ppermute | solution.py:50
  491.8 45.9 %collective-permute-start.47 = (bf16[128,1408]{1,0:T(8,128)(2,1)}, bf16[128,1408]{1,0:T(8,128)(2,1)}, u32[]{:S(2)}, u32[]{:S(2)}) collective-permute-start(bf16[128,1408]{1,0:T(8,128)(2,1)} %constant_dynamic-slice_fusion.51), channel_id=1, source_target_pairs={{0,8},{8,0},{1,9},{9,1},{2,10},{10,2},{3,11},{11,3},{4,12},{12,4},... | collective-permute-start | bytes 1081352 | tf_op jit(solution)/shard_map/ppermute | solution.py:50
  492.9 45.9 %collective-permute-start.48 = (bf16[128,1408]{1,0:T(8,128)(2,1)}, bf16[128,1408]{1,0:T(8,128)(2,1)}, u32[]{:S(2)}, u32[]{:S(2)}) collective-permute-start(bf16[128,1408]{1,0:T(8,128)(2,1)} %constant_dynamic-slice_fusion.50), channel_id=1, source_target_pairs={{0,4},{4,0},{1,5},{5,1},{2,6},{6,2},{3,7},{7,3},{8,12},{12,8},{9,1... | collective-permute-start | bytes 1081352 | tf_op jit(solution)/shard_map/ppermute | solution.py:50
  533.9 89.9 %collective-permute-start.51 = (bf16[512,1024]{1,0:T(8,128)(2,1)}, bf16[512,1024]{1,0:T(8,128)(2,1)}, u32[]{:S(2)}, u32[]{:S(2)}) collective-permute-start(bf16[512,1024]{1,0:T(8,128)(2,1)} %pad_maximum_fusion.20), channel_id=1, source_target_pairs={{0,4},{4,0},{1,5},{5,1},{2,6},{6,2},{3,7},{7,3},{8,12},{12,8},{9,1... | collective-permute-start | bytes 3145736 | tf_op jit(solution)/shard_map/ppermute | solution.py:50
  534.5 91.4 %collective-permute-start.52 = (bf16[512,1024]{1,0:T(8,128)(2,1)}, bf16[512,1024]{1,0:T(8,128)(2,1)}, u32[]{:S(2)}, u32[]{:S(2)}) collective-permute-start(bf16[512,1024]{1,0:T(8,128)(2,1)} %pad_maximum_fusion.21), channel_id=1, source_target_pairs={{0,8},{8,0},{1,9},{9,1},{2,10},{10,2},{3,11},{11,3},{4,12},{12,4},... | collective-permute-start | bytes 3145736 | tf_op jit(solution)/shard_map/ppermute | solution.py:50
  576.7 39.9 %collective-permute-start.57 = (bf16[256,640]{1,0:T(8,128)(2,1)}, bf16[256,640]{1,0:T(8,128)(2,1)}, u32[]{:S(2)}, u32[]{:S(2)}) collective-permute-start(bf16[256,640]{1,0:T(8,128)(2,1)} %get-tuple-element.410), channel_id=1, source_target_pairs={{0,2},{1,3},{2,0},{3,1},{4,6},{5,7},{6,4},{7,5},{8,10},{9,11},{10,... | collective-permute-start | bytes 983048 | tf_op jit(solution)/shard_map/ppermute | solution.py:50
  579.9 38.7 %collective-permute-start.56 = (bf16[256,640]{1,0:T(8,128)(2,1)}, bf16[256,640]{1,0:T(8,128)(2,1)S(1)}, u32[]{:S(2)}, u32[]{:S(2)}) collective-permute-start(bf16[256,640]{1,0:T(8,128)(2,1)} %get-tuple-element.409), channel_id=1, source_target_pairs={{0,1},{1,2},{2,3},{3,0},{4,5},{5,6},{6,7},{7,4},{8,9},{9,10},{10,1... | collective-permute-start | bytes 983048 | tf_op jit(solution)/shard_map/ppermute | solution.py:50
  592.8 40.8 %collective-permute-start.65 = (bf16[256,1024]{1,0:T(8,128)(2,1)}, bf16[256,1024]{1,0:T(8,128)(2,1)S(1)}, u32[]{:S(2)}, u32[]{:S(2)}) collective-permute-start(bf16[256,1024]{1,0:T(8,128)(2,1)} %get-tuple-element.248), channel_id=1, source_target_pairs={{16,17},{17,18},{18,19},{19,16},{20,21},{21,22},{22,23},{23,20},{2... | collective-permute-start | bytes 1572872 | tf_op jit(solution)/shard_map/ppermute | solution.py:114
  655.3 46.6 %collective-permute-start.62 = (bf16[256,1024]{1,0:T(8,128)(2,1)}, bf16[256,1024]{1,0:T(8,128)(2,1)}, u32[]{:S(2)}, u32[]{:S(2)}) collective-permute-start(bf16[256,1024]{1,0:T(8,128)(2,1)} %get-tuple-element.236), channel_id=1, source_target_pairs={{0,1},{1,2},{2,3},{3,0},{4,5},{5,6},{6,7},{7,4},{8,9},{9,10},{10,1... | collective-permute-start | bytes 1572872 | tf_op jit(solution)/shard_map/ppermute | solution.py:114
  656.8 52.8 %collective-permute-start.63 = (bf16[256,1024]{1,0:T(8,128)(2,1)}, bf16[256,1024]{1,0:T(8,128)(2,1)}, u32[]{:S(2)}, u32[]{:S(2)}) collective-permute-start(bf16[256,1024]{1,0:T(8,128)(2,1)} %get-tuple-element.235), channel_id=1, source_target_pairs={{0,2},{1,3},{2,0},{3,1},{4,6},{5,7},{6,4},{7,5},{8,10},{9,11},{10,... | collective-permute-start | bytes 1572872 | tf_op jit(solution)/shard_map/ppermute | solution.py:114
  667.7 29.0 %collective-permute-start.78 = (bf16[256,512]{1,0:T(8,128)(2,1)}, bf16[256,512]{1,0:T(8,128)(2,1)}, u32[]{:S(2)}, u32[]{:S(2)}) collective-permute-start(bf16[256,512]{1,0:T(8,128)(2,1)} %pad_maximum_fusion.51), channel_id=1, source_target_pairs={{0,2},{1,3},{2,0},{3,1},{4,6},{5,7},{6,4},{7,5},{8,10},{9,11},{10,... | collective-permute-start | bytes 786440 | tf_op jit(solution)/shard_map/ppermute | solution.py:50
  673.8 37.0 %collective-permute-start.64 = (bf16[256,1024]{1,0:T(8,128)(2,1)}, bf16[256,1024]{1,0:T(8,128)(2,1)S(1)}, u32[]{:S(2)}, u32[]{:S(2)}) collective-permute-start(bf16[256,1024]{1,0:T(8,128)(2,1)} %get-tuple-element.234), channel_id=1, source_target_pairs={{0,3},{1,0},{2,1},{3,2},{4,7},{5,4},{6,5},{7,6},{8,11},{9,8},{10,9... | collective-permute-start | bytes 1572872 | tf_op jit(solution)/shard_map/ppermute | solution.py:114
  701.8 56.8 %collective-permute-start.80 = (f32[256,512]{1,0:T(8,128)}, f32[256,512]{1,0:T(8,128)S(1)}, u32[]{:S(2)}, u32[]{:S(2)}) collective-permute-start(f32[256,512]{1,0:T(8,128)} %get-tuple-element.298), channel_id=1, source_target_pairs={{0,16},{16,0},{1,17},{17,1},{2,18},{18,2},{3,19},{19,3},{4,20},{20... | collective-permute-start | bytes 1572872 | tf_op jit(solution)/shard_map/ppermute | solution.py:98
  723.2 28.1 %collective-permute-start.75 = (bf16[288,640]{1,0:T(8,128)(2,1)S(1)}, bf16[288,640]{1,0:T(8,128)(2,1)S(1)}, u32[]{:S(2)}, u32[]{:S(2)}) collective-permute-start(bf16[288,640]{1,0:T(8,128)(2,1)S(1)} %get-tuple-element.407), channel_id=1, source_target_pairs={{0,2},{1,3},{2,0},{3,1},{4,6},{5,7},{6,4},{7,5},{8,10},{9,11},{10,... | collective-permute-start | bytes 1105928 | tf_op jit(solution)/shard_map/ppermute | solution.py:50
  724.1 27.2 %collective-permute-start.74 = (bf16[288,640]{1,0:T(8,128)(2,1)S(1)}, bf16[288,640]{1,0:T(8,128)(2,1)S(1)}, u32[]{:S(2)}, u32[]{:S(2)}) collective-permute-start(bf16[288,640]{1,0:T(8,128)(2,1)S(1)} %get-tuple-element.406), channel_id=1, source_target_pairs={{0,1},{1,2},{2,3},{3,0},{4,5},{5,6},{6,7},{7,4},{8,9},{9,10},{10,1... | collective-permute-start | bytes 1105928 | tf_op jit(solution)/shard_map/ppermute | solution.py:50
  (227 other events, 3110.2 us)
where the time goes:
time: 779 us; the launch traced here: 773 us
  waiting for transfers between devices  249 us (32%)
  starting transfers between devices  136 us (17%)
  Pallas kernels  113 us (15%)
  other arithmetic  95.8 us (12%)
  local copies, waits for them, and re-layouts  89.3 us (11%)
  matrix products  84.3 us (11%)
    ppermute x55, waiting for transfers between devices, rotated(): lax.ppermute(value, axis, [(i, (i + steps) % count) for i in range(count)])  228 us
    pallas_call x2, Pallas kernels, ssm_backward(): pl.pallas_call(bwd_kernel, grid=(blocks,), in_specs=[pl.BlockSpec((CHUNK,...  68.6 us
    ppermute x55, starting transfers between devices, rotated(): lax.ppermute(value, axis, [(i, (i + steps) % count) for i in range(count)])  54.6 us
    dot_general x10, matrix products, dot_nn(): lax.dot_general(a, b, (((1,), (0,)), ((), ())), precision=precision, pref...  37 us
    ppermute x9, starting transfers between devices, spread_rows(): arrived = lax.ppermute(block, ('section', 'tp'), pairs)  36.6 us
    ppermute x10, starting transfers between devices, swap_cores(): return lax.ppermute(value, 'section', [(0, 1), (1, 0)])  27.1 us
    dot_general x8, matrix products, dot_tn(): lax.dot_general(a, b, (((0,), (0,)), ((), ())), precision=precision, pref...  25.9 us
    unnamed x394, local copies, waits for them, and re-layouts  25.8 us
  transfers between devices with their start and end apart: 82, of which 29 were waited for; matrix products, arithmetic and copies ran while one was open for 22% of the time, Pallas kernels for 15%

commit v1 on v0

--- a/solution.py
+++ b/solution.py
@@ -70,12 +70,13 @@
     return lax.dynamic_slice_in_dim(line, count - 1 - place, count, dim)
 
 
-def ring_gather(value, axis):
-    count = lax.axis_size(axis)
-    place = lax.axis_index(axis)
-    came = [value] + [rotated(value, axis, steps) for steps in range(1, count)]
-    line = jnp.stack(came[::-1] + came[:0:-1])
-    return lax.dynamic_slice_in_dim(line, count - 1 - place, count, 0)
+def tp_gather(value):
+    copies = jnp.broadcast_to(value, (lax.axis_size("tp"),) + value.shape)
+    return lax.all_to_all(copies, "tp", 0, 0)
+
+
+def tp_sum(blocks):
+    return jnp.sum(lax.all_to_all(blocks, "tp", 0, 0).astype(full), axis=0)
 
 
 def scatter_sum(pick, axis):
@@ -98,22 +99,9 @@
     return lax.ppermute(value, "section", [(0, 1), (1, 0)])
 
 
-def spread_rows(value, pairs_of):
+def spread_rows(value):
     count = lax.axis_size("tp")
-    place = lax.axis_index("tp")
-    result = jnp.zeros_like(value)
-    own = lax.dynamic_index_in_dim(value, place, 0, False)
-    result = lax.dynamic_update_index_in_dim(result, own, place, 0)
-    for steps in range(1, count):
-        block = lax.dynamic_index_in_dim(value, (place + steps) % count, 0, False)
-        pairs = [
-            (core * count + i, core * count + (i + steps) % count)
-            for core in pairs_of
-            for i in range(count)
-        ]
-        arrived = lax.ppermute(block, ("section", "tp"), pairs)
-        result = lax.dynamic_update_index_in_dim(result, arrived, (place - steps) % count, 0)
-    return result
+    return lax.all_to_all(value.reshape(count, value.shape[0] // count, value.shape[1]), "tp", 0, 0)
 
 
 def gather_rows(early, late):
@@ -573,9 +561,8 @@
     back_normed = dot_nn(back_branch, out_weight)
     if pending is not None:
         pair, feed = pending
-        back_normed, (pair.sums, feed.sums) = tied(back_normed, (pair.sums, feed.sums))
+        back_normed, pair.sums = tied(back_normed, pair.sums)
         pair.sums = pair_sum(pair.sums)
-        feed.second()
     back_wide = back_branch.astype(full)
     grad_out = dot_tn((back_wide * out_norm).astype(low), scaled).astype(low)
     along = jnp.sum(back_wide * branch.astype(full), axis=-1, keepdims=True)
@@ -593,7 +580,7 @@
     early = whole_reduction(grad_gate, grad_out)
     if pending is not None:
         back_ssm, feed.sums = tied(back_ssm, feed.sums)
-        feed.sums = feed_sum(feed.sums, inner)
+        feed.second()
     early.first()
     back_all, first_rows, sums, head_sums = ssm_backward(*scan, back_ssm, starts, later, *conv)
     following = shifted(first_rows, "ctx", -1)
@@ -607,6 +594,7 @@
     back_all, early.sums = tied(back_all, early.sums)
     if pending is not None:
         back_all, (pair.sums, feed.sums) = tied(back_all, (pair.sums, feed.sums))
+        feed.sums = feed_sum(feed.sums, inner)
     early.second()
     grad_skip = jnp.sum(sums[CONV + 1, :inner].reshape(heads, HEADDIM), axis=1)
     grad_step_bias, grad_decay = head_sums[0, :heads], head_sums[1, :heads]
@@ -674,25 +662,24 @@
     return Reduction((array, 0, rows // 2), (array, rows // 2, rows))
 
 
-def lanes_of(value, at, inner):
+def lane_blocks(value, inner):
     each = inner // lax.axis_size("tp")
-    return lax.dynamic_slice_in_dim(value, at * each, each, 1)
+    return jnp.stack([value[:, at : at + each] for at in range(0, inner, each)])
 
 
 def pair_sum(sums):
-    return scatter_sum(lambda at: columns(lanes_of(part, at, part.shape[1]) for part in sums), "tp")
+    return tp_sum(columns(lane_blocks(part, part.shape[1]) for part in sums))
 
 
 def feed_sum(sums, inner, small=None):
     joined = jnp.concatenate(sums, axis=0)
-
-    def pick(at):
-        block = columns([lanes_of(joined, at, inner), joined[:, inner:]])
-        if small is not None:
-            block = jnp.concatenate([block, as_rows(small, block.shape[1])], axis=0)
-        return block
-
-    return scatter_sum(pick, "tp")
+    rest = joined[:, inner:]
+    count = lax.axis_size("tp")
+    blocks = columns([lane_blocks(joined, inner), jnp.broadcast_to(rest, (count,) + rest.shape)])
+    if small is not None:
+        extra = as_rows(small, blocks.shape[2])
+        blocks = jnp.concatenate([blocks, jnp.broadcast_to(extra, (count,) + extra.shape)], axis=1)
+    return tp_sum(blocks)
 
 
 def on_device(
@@ -808,13 +795,14 @@
     smalls = both_layers(pack_small)
     packs = both_layers(pack)
     feed_sections, pair_sections = (half, quarter, wide), (half, half)
-    along_feed = ring_gather(jnp.concatenate([packs[0][:, :cut], smalls[0]], axis=0), "tp")
+    along_feed = tp_gather(jnp.concatenate([packs[0][:, :cut], smalls[0]], axis=0))
     pair_pack, along_feed = tied(packs[0][:, cut:], along_feed)
-    along_pair = ring_gather(pair_pack, "tp")
+    along_pair = tp_gather(pair_pack)
     feed_parts = gather_item(along_feed[:, :own_rows], feed_sections)
-    last_pack, along_pair = tied(packs[1], along_pair)
+    last_pack, along_feed = tied(packs[1], along_feed)
+    along_pair, feed_parts = tied(along_pair, feed_parts)
     small_pad = jnp.pad(smalls[1], ((0, 0), (0, last_pack.shape[1] - cut)))
-    along_last = ring_gather(jnp.concatenate([last_pack, small_pad], axis=0), "tp")
+    along_last = tp_gather(jnp.concatenate([last_pack, small_pad], axis=0))
     pair_parts = gather_item(along_pair, pair_sections)
     along_last, pair_parts = tied(along_last, pair_parts)
     last_parts = gather_item(along_last[:, :own_rows, :cut], feed_sections)
@@ -843,14 +831,19 @@
     result_last, kept_last = layer_forward(low_first.astype(full), before, valid, weights[1], params[1])
     own_result = jnp.where(first, low_first, result_last.astype(low))
     quarter_rows = rows // tp_count
-    section_out = spread_rows(own_result.reshape(tp_count, quarter_rows, width), (0, 1))
+    section_out = spread_rows(own_result)
+
+    column = core * (width // 2)
+
+    def half_columns(value):
+        return lax.dynamic_slice_in_dim(value.astype(low), column, width // 2, 1)
 
     delta_last, feed_last, small_last, pair_last = layer_backward(
         out_grad, valid, weights[1], params[1], kept_last
     )
     last = split_reduction(feed_last)
     last.first()
-    spread_last = spread_rows(delta_last.astype(low).reshape(tp_count, quarter_rows, width), (1,))
+    spread_last = spread_rows(half_columns(delta_last))
     incoming = (out_grad + delta_last).astype(low).astype(full)
     delta_first, feed_first, small_first, pair_first = layer_backward(
         incoming, valid, weights[0], params[0], kept_first, (pair_last, last)
@@ -861,16 +854,19 @@
     feed.first()
     pair_first_sum = pair_sum(pair_first.sums)
     small = jnp.stack([small_first, small_last])
-    spread_first = spread_rows(grad_first.reshape(tp_count, quarter_rows, width), (0,))
+    spread_first = spread_rows(half_columns(grad_first))
     small = all_sum(all_sum(small, "ctx"), "dp")
     feed.second()
     feed_sums = feed_sum(feed.sums, inner, small.astype(low).reshape(-1))
     own_cotangent = lax.dynamic_slice_in_dim(
         cotangent[:, 0], lane * quarter_rows, quarter_rows, 1
     )
-    input_grad = jnp.where(
-        first, spread_first.astype(full), own_cotangent + spread_last.astype(full)
-    )
+    spread_keep = jnp.where(first, spread_first, spread_last)
+    spread_came = swap_cores(jnp.where(first, spread_last, spread_first))
+    spread = columns(
+        [jnp.where(first, spread_keep, spread_came), jnp.where(first, spread_came, spread_keep)]
+    ).astype(full)
+    input_grad = jnp.where(first, spread, own_cotangent + spread)
 
     pair_keep = jnp.where(first, pair_first_sum, pair_last.sums)
     pair_came = swap_cores(jnp.where(first, pair_last.sums, pair_first_sum))

time: 779 us -> 807 us (1.036)
  other arithmetic: 95.8 us -> 138 us
  starting transfers between devices: 136 us -> 108 us
  local copies, waits for them, and re-layouts: 89.3 us -> 114 us
  waiting for transfers between devices: 249 us -> 232 us
    ppermute x55 -> x34, waiting for transfers between devices: 228 us -> 82.5 us  [rotated(): lax.ppermute(value, axis, [(i, (i + steps) % count) for i in range(count)])]
    all_to_all x0 -> x10, waiting for transfers between devices: none -> 124 us  [the longest x4 64.6 us: tp_sum(): return jnp.sum(lax.all_to_all(blocks, 'tp', 0, 0).astype(full), axis=0)]
    all_to_all x0 -> x10, starting transfers between devices: none -> 42.9 us  [the longest x4 17.4 us: tp_sum(): return jnp.sum(lax.all_to_all(blocks, 'tp', 0, 0).astype(full), axis=0)]
    ppermute x9 -> x0, starting transfers between devices: 36.6 us -> none  [spread_rows(): arrived = lax.ppermute(block, ('section', 'tp'), pairs)]
    ppermute x55 -> x34, starting transfers between devices: 54.6 us -> 27.2 us  [rotated(): lax.ppermute(value, axis, [(i, (i + steps) % count) for i in range(count)])]
    unnamed x394 -> x441, local copies, waits for them, and re-layouts: 25.8 us -> 42.5 us
    dynamic_update_slice x10 -> x0, local copies, waits for them, and re-layouts: 8.12 us -> none  [the longest x9 8.08 us: spread_rows(): lax.dynamic_update_index_in_dim(result, arrived, (place - steps) % count, 0)]
    ppermute x10 -> x11, starting transfers between devices: 27.1 us -> 19.2 us  [swap_cores(): return lax.ppermute(value, 'section', [(0, 1), (1, 0)])]
  transfers between devices with their start and end apart: 82 -> 63, of which waited for: 29 -> 27; matrix products, arithmetic and copies ran while one was open for 22% -> 27% of each run, Pallas kernels for 15% -> 14%
where the time goes in v1:
time: 807 us; the launch traced here: 798 us
  waiting for transfers between devices  232 us (29%)
  other arithmetic  138 us (17%)
  local copies, waits for them, and re-layouts  114 us (14%)
  Pallas kernels  114 us (14%)
  starting transfers between devices  108 us (13%)
  matrix products  86.7 us (11%)
    ppermute x34, waiting for transfers between devices, rotated(): lax.ppermute(value, axis, [(i, (i + steps) % count) for i in range(count)])  82.5 us
    pallas_call x2, Pallas kernels, ssm_backward(): pl.pallas_call(bwd_kernel, grid=(blocks,), in_specs=[pl.BlockSpec((CHUNK,...  69.7 us
    all_to_all x4, waiting for transfers between devices, tp_sum(): return jnp.sum(lax.all_to_all(blocks, 'tp', 0, 0).astype(full), axis=0)  64.6 us
    all_to_all x3, waiting for transfers between devices, spread_rows(): lax.all_to_all(value.reshape(count, value.shape[0] // count, value.shape[...  44.6 us
    unnamed x441, local copies, waits for them, and re-layouts  42.5 us
    dot_general x10, matrix products, dot_nn(): lax.dot_general(a, b, (((1,), (0,)), ((), ())), precision=precision, pref...  37.6 us
    ppermute x34, starting transfers between devices, rotated(): lax.ppermute(value, axis, [(i, (i + steps) % count) for i in range(count)])  27.2 us
    dot_general x8, matrix products, dot_tn(): lax.dot_general(a, b, (((0,), (0,)), ((), ())), precision=precision, pref...  25.8 us
  transfers between devices with their start and end apart: 63, of which 27 were waited for; matrix products, arithmetic and copies ran while one was open for 27% of the time, Pallas kernels for 14%

profile of v1, /device:TPU:1, one launch (start us, length us, event | category | flops | bytes accessed | tf_op | source)
XLA Modules:
  0.0 797.8 jit_solution(16854383403077586433)
XLA Ops:
  7.7 5.9 all-to-all-start
  20.2 15.3 %all-to-all-done = bf16[4,288,384]{2,1,0:T(8,128)(2,1)S(1)} async-done(((bf16[4,288,384]{2,1,0:T(8,128)(2,1)}), bf16[4,288,384]{2,1,0:T(8,128)(2,1)S(1)}, u32[]{:S(2)}, u32[]{:S(2)}) %all-to-all-start) | async-done | bytes 884768 | tf_op jit(solution)/shard_map/all_to_all | solution.py:75
  46.5 6.2 collective-permute-done.2
  59.6 12.3 %collective-permute-done.3 = bf16[2,256,768]{2,1,0:T(8,128)(2,1)} collective-permute-done((bf16[2,256,768]{2,1,0:T(8,128)(2,1)}, bf16[2,256,768]{2,1,0:T(8,128)(2,1)}, u32[]{:S(2)}, u32[]{:S(2)}) %collective-permute-start.3) | collective-permute-done | bytes 786464 | tf_op jit(solution)/shard_map/ppermute | solution.py:50
  100.8 5.9 fusion.164
  114.9 9.7 %mixer_prep.2 = (f32[1024,1280]{1,0:T(8,128)S(1)}, f32[1024,128]{1,0:T(8,128)S(1)}, f32[1024,128]{1,0:T(8,128)S(1)}, f32[16,1024]{1,0:T(8,128)S(1)}, f32[1024,128]{1,0:T(8,128)S(1)}, /*index=5*/f32[1024,128]{1,0:T(8,128)S(1)}) custom-call(bf16[1024,1280]{1,0:T(8,128)(2,1)S(1)} %slice.1031.feed_ref.before_ref, bf16[16,1280]{1,0:T(8,128)(2,1)S(1)} %fusion.50.rim_ref, ...), custom_call_target="tpu_custom_call" | custom-call | flops 268435456 | bytes 7864320 | tf_op jit(solution)/shard_map/mixer_prep/pallas_call | solution.py:183
  139.4 12.7 %ssm_forward.2 = (f32[1024,1024]{1,0:T(8,128)S(1)}, bf16[8,1024,128]{2,1,0:T(8,128)(2,1)S(1)}) custom-call(f32[1024,1280]{1,0:T(8,128)S(1)} %copy-done.3, f32[1024,1280]{1,0:T(8,128)S(1)} %copy-done.3, f32[1024,128]{1,0:T(8,128)S(1)} %get-tuple-element.90.dt_ref, f32[1024,128]{1,0:T(8,128)S(1)} %get-tuple-element.91.cum_ref, ...), custom_call_target="tpu_custom_call" | custom-call | flops 1073741824 | bytes 10485760 | tf_op jit(solution)/shard_map/ssm_forward/pallas_call | solution.py:389
  173.1 8.4 %multiply_reduce_fusion.3 = (f32[1024]{0:T(1024)S(1)}, f32[1024,1024]{1,0:T(8,128)S(1)}, f32[1024,1024]{1,0:T(8,128)}) fusion(f32[1024,1024]{1,0:T(8,128)} %copy-done.11, bf16[1024,1024]{1,0:T(8,128)(2,1)} %constant_dynamic-update-slice_fusion.8, f32[1024]{0:T(1024)S(1)} %convert_reduce_fusion.5, f32[1024]{0:T(1024)S(1)} %add_rsqrt_fusion.3, ...), kind=kOutput, calls=%fused_computation.66 | convolution fusion | flops 2159016960 | bytes 16789508 | tf_op jit(solution)/shard_map/dot_general | solution.py:25
  200.3 12.0 %collective-permute-done.17 = bf16[2,256,768]{2,1,0:T(8,128)(2,1)S(1)} collective-permute-done((bf16[2,256,768]{2,1,0:T(8,128)(2,1)S(1)}, bf16[2,256,768]{2,1,0:T(8,128)(2,1)S(1)}, u32[]{:S(2)}, u32[]{:S(2)}) %collective-permute-start.17) | collective-permute-done | bytes 786464 | tf_op jit(solution)/shard_map/ppermute | solution.py:50
  243.3 8.7 %collective-permute-done.18 = bf16[16,1024]{1,0:T(8,128)(2,1)S(1)} collective-permute-done((bf16[16,1024]{1,0:T(8,128)(2,1)S(1)}, bf16[16,1024]{1,0:T(8,128)(2,1)S(1)}, u32[]{:S(2)}, u32[]{:S(2)}) %collective-permute-start.18) | collective-permute-done | bytes 32800 | tf_op jit(solution)/shard_map/ppermute | solution.py:45
  252.7 9.7 %mixer_prep.3 = (f32[1024,1280]{1,0:T(8,128)S(1)}, f32[1024,128]{1,0:T(8,128)S(1)}, f32[1024,128]{1,0:T(8,128)S(1)}, f32[16,1024]{1,0:T(8,128)S(1)}, f32[1024,128]{1,0:T(8,128)S(1)}, /*index=5*/f32[1024,128]{1,0:T(8,128)S(1)}) custom-call(bf16[1024,1280]{1,0:T(8,128)(2,1)S(1)} %slice.1030.feed_ref.before_ref, bf16[16,1280]{1,0:T(8,128)(2,1)S(1)} %fusion.47.rim_ref, ...), custom_call_target="tpu_custom_call" | custom-call | flops 268435456 | bytes 7864320 | tf_op jit(solution)/shard_map/mixer_prep/pallas_call | solution.py:183
  270.7 12.2 %ssm_forward.3 = (f32[1024,1024]{1,0:T(8,128)S(1)}, bf16[8,1024,128]{2,1,0:T(8,128)(2,1)S(1)}) custom-call(f32[1024,1280]{1,0:T(8,128)S(1)} %get-tuple-element.109.x_ref.bc_ref, f32[1024,1280]{1,0:T(8,128)S(1)} %get-tuple-element.109.x_ref.bc_ref, f32[1024,128]{1,0:T(8,128)S(1)} %get-tuple-element.110.dt_ref, f32[1024,128]{1,0:T(8,128)S(1)} %get-tuple-element.111.cum_ref, ...), custom_call_target="tpu_custom_call" | custom-call | flops 1073741824 | bytes 10485760 | tf_op jit(solution)/shard_map/ssm_forward/pallas_call | solution.py:389
  306.5 5.1 fusion
  312.4 7.2 fusion.58
  341.8 5.0 fusion.30
  346.9 34.4 %ssm_backward.2 = (bf16[1024,1408]{1,0:T(8,128)(2,1)S(1)}, f32[8,1280]{1,0:T(8,128)}, f32[8,1280]{1,0:T(8,128)S(1)}, f32[8,128]{1,0:T(8,128)S(1)}) custom-call(f32[1024,1280]{1,0:T(8,128)} %copy-done.4, f32[1024,1280]{1,0:T(8,128)} %copy-done.4, f32[1024,128]{1,0:T(8,128)S(1)} %copy-done.22, f32[1024,128]{1,0:T(8,128)S(1)} %copy-done.24, ...), custom_call_target="tpu_custom_call" | custom-call | flops 4294967296 | bytes 16777216 | tf_op jit(solution)/shard_map/ssm_backward/pallas_call | solution.py:432
  407.7 9.9 %collective-permute-done.31 = bf16[256,1024]{1,0:T(8,128)(2,1)S(1)} collective-permute-done((bf16[256,1024]{1,0:T(8,128)(2,1)S(1)}, bf16[256,1024]{1,0:T(8,128)(2,1)S(1)}, u32[]{:S(2)}, u32[]{:S(2)}) %collective-permute-start.31) | collective-permute-done | bytes 524320 | tf_op jit(solution)/shard_map/ppermute | solution.py:50
  418.5 15.2 %collective-permute-done.33 = bf16[256,1408]{1,0:T(8,128)(2,1)S(1)} collective-permute-done((bf16[256,1408]{1,0:T(8,128)(2,1)S(1)}, bf16[256,1408]{1,0:T(8,128)(2,1)S(1)}, u32[]{:S(2)}, u32[]{:S(2)}) %collective-permute-start.33) | collective-permute-done | bytes 720928 | tf_op jit(solution)/shard_map/ppermute | solution.py:50
  438.2 6.1 fusion.4
  474.1 5.1 all-to-all-start.4
  494.0 35.2 %ssm_backward.3 = (bf16[1024,1408]{1,0:T(8,128)(2,1)S(1)}, f32[8,1280]{1,0:T(8,128)}, f32[8,1280]{1,0:T(8,128)S(1)}, f32[8,128]{1,0:T(8,128)S(1)}) custom-call(f32[1024,1280]{1,0:T(8,128)} %copy-done.2, f32[1024,1280]{1,0:T(8,128)} %copy-done.2, f32[1024,128]{1,0:T(8,128)S(1)} %copy-done.18, f32[1024,128]{1,0:T(8,128)S(1)} %copy-done.20, ...), custom_call_target="tpu_custom_call" | custom-call | flops 4294967296 | bytes 16777216 | tf_op jit(solution)/shard_map/ssm_backward/pallas_call | solution.py:432
  554.6 5.4 fusion.186
  570.7 10.0 %collective-permute-done.43 = bf16[256,1024]{1,0:T(8,128)(2,1)S(1)} collective-permute-done((bf16[256,1024]{1,0:T(8,128)(2,1)S(1)}, bf16[256,1024]{1,0:T(8,128)(2,1)S(1)}, u32[]{:S(2)}, u32[]{:S(2)}) %collective-permute-start.43) | collective-permute-done | bytes 524320 | tf_op jit(solution)/shard_map/ppermute | solution.py:50
  581.7 5.0 convolution_convert_fusion
  589.3 10.8 %all-to-all-done.3 = bf16[4,256,1024]{2,1,0:T(8,128)(2,1)} async-done(((bf16[4,256,1024]{2,1,0:T(8,128)(2,1)}), bf16[4,256,1024]{2,1,0:T(8,128)(2,1)}, u32[]{:S(2)}, u32[]{:S(2)}) %all-to-all-start.3) | async-done | bytes 2097184 | tf_op jit(solution)/shard_map/all_to_all | solution.py:104
  613.7 15.1 %all-to-all-done.6 = bf16[4,256,512]{2,1,0:T(8,128)(2,1)S(1)} async-done(((bf16[4,256,512]{2,1,0:T(8,128)(2,1)}), bf16[4,256,512]{2,1,0:T(8,128)(2,1)S(1)}, u32[]{:S(2)}, u32[]{:S(2)}) %all-to-all-start.6) | async-done | bytes 1048608 | tf_op jit(solution)/shard_map/all_to_all | solution.py:104
  635.1 28.3 %all-to-all-done.8 = bf16[4,256,640]{2,1,0:T(8,128)(2,1)S(1)} async-done(((bf16[4,256,640]{2,1,0:T(8,128)(2,1)}), bf16[4,256,640]{2,1,0:T(8,128)(2,1)S(1)}, u32[]{:S(2)}, u32[]{:S(2)}) %all-to-all-start.8) | async-done | bytes 1310752 | tf_op jit(solution)/shard_map/all_to_all | solution.py:79
  673.4 18.6 %all-to-all-done.5 = bf16[4,256,512]{2,1,0:T(8,128)(2,1)S(1)} async-done(((bf16[4,256,512]{2,1,0:T(8,128)(2,1)}), bf16[4,256,512]{2,1,0:T(8,128)(2,1)S(1)}, u32[]{:S(2)}, u32[]{:S(2)}) %all-to-all-start.5) | async-done | bytes 1048608 | tf_op jit(solution)/shard_map/all_to_all | solution.py:104
  699.5 6.5 collective-permute-done.46
  708.5 13.1 %all-to-all-done.9 = bf16[4,256,512]{2,1,0:T(8,128)(2,1)} async-done(((bf16[4,256,512]{2,1,0:T(8,128)(2,1)}), bf16[4,256,512]{2,1,0:T(8,128)(2,1)}, u32[]{:S(2)}, u32[]{:S(2)}) %all-to-all-start.9) | async-done | bytes 1048608 | tf_op jit(solution)/shard_map/all_to_all | solution.py:79
  737.1 23.2 %all-to-all-done.7 = bf16[4,288,640]{2,1,0:T(8,128)(2,1)} async-done(((bf16[4,288,640]{2,1,0:T(8,128)(2,1)}), bf16[4,288,640]{2,1,0:T(8,128)(2,1)}, u32[]{:S(2)}, u32[]{:S(2)}) %all-to-all-start.7) | async-done | bytes 1474592 | tf_op jit(solution)/shard_map/all_to_all | solution.py:79
  769.6 5.3 add_select_fusion
  (901 shorter events, 409.4 us)
Async XLA Ops:
  7.7 27.8 %all-to-all-start = ((bf16[4,288,384]{2,1,0:T(8,128)(2,1)}), bf16[4,288,384]{2,1,0:T(8,128)(2,1)S(1)}, u32[]{:S(2)}, u32[]{:S(2)}) async-start(bf16[4,288,384]{2,1,0:T(8,128)(2,1)} %broadcast_in_dim.38), calls=%async_computation | async-start | bytes 1769472 | tf_op jit(solution)/shard_map/all_to_all | solution.py:75
  39.5 39.5 %all-to-all-start.1 = ((bf16[4,256,512]{2,1,0:T(8,128)(2,1)}), bf16[4,256,512]{2,1,0:T(8,128)(2,1)S(1)}, u32[]{:S(2)}, u32[]{:S(2)}) async-start(bf16[4,256,512]{2,1,0:T(8,128)(2,1)} %broadcast_in_dim.78), calls=%async_computation.1 | async-start | bytes 2097152 | tf_op jit(solution)/shard_map/all_to_all | solution.py:75
  80.5 79.9 %all-to-all-start.2 = ((bf16[4,288,896]{2,1,0:T(8,128)(2,1)}), bf16[4,288,896]{2,1,0:T(8,128)(2,1)S(1)}, u32[]{:S(2)}, u32[]{:S(2)}) async-start(bf16[4,288,896]{2,1,0:T(8,128)(2,1)} %broadcast_in_dim.80), calls=%async_computation.2 | async-start | bytes 4128768 | tf_op jit(solution)/shard_map/all_to_all | solution.py:75
  87.4 23.5 %collective-permute-start.8 = (bf16[256,1024]{1,0:T(8,128)(2,1)}, bf16[256,1024]{1,0:T(8,128)(2,1)}, u32[]{:S(2)}, u32[]{:S(2)}) collective-permute-start(bf16[256,1024]{1,0:T(8,128)(2,1)} %pad_maximum_fusion.34), channel_id=1, source_target_pairs={{0,4},{4,0},{1,5},{5,1},{2,6},{6,2},{3,7},{7,3},{8,12},{12,8},{9,1... | collective-permute-start | bytes 1572872 | tf_op jit(solution)/shard_map/ppermute | solution.py:50
  110.6 41.7 %collective-permute-start.11 = (bf16[2,256,1024]{2,1,0:T(8,128)(2,1)}, bf16[2,256,1024]{2,1,0:T(8,128)(2,1)}, u32[]{:S(2)}, u32[]{:S(2)}) collective-permute-start(bf16[2,256,1024]{2,1,0:T(8,128)(2,1)} %pad_maximum_fusion.17), channel_id=1, source_target_pairs={{0,4},{4,0},{1,5},{5,1},{2,6},{6,2},{3,7},{7,3},{8,12},{12,8},{9,1... | collective-permute-start | bytes 3145736 | tf_op jit(solution)/shard_map/ppermute | solution.py:50
  113.5 41.6 %collective-permute-start.9 = (bf16[2,256,1024]{2,1,0:T(8,128)(2,1)}, bf16[2,256,1024]{2,1,0:T(8,128)(2,1)}, u32[]{:S(2)}, u32[]{:S(2)}) collective-permute-start(bf16[2,256,1024]{2,1,0:T(8,128)(2,1)} %pad_maximum_fusion.16), channel_id=1, source_target_pairs={{0,8},{8,0},{1,9},{9,1},{2,10},{10,2},{3,11},{11,3},{4,12},{12,4},... | collective-permute-start | bytes 3145736 | tf_op jit(solution)/shard_map/ppermute | solution.py:50
  188.7 43.5 %collective-permute-start.13 = (bf16[1024,1024]{1,0:T(8,128)(2,1)}, bf16[1024,1024]{1,0:T(8,128)(2,1)}, u32[]{:S(2)}, u32[]{:S(2)}) collective-permute-start(bf16[1024,1024]{1,0:T(8,128)(2,1)} %convolution_convert_fusion.5), channel_id=1, source_target_pairs={{0,16},{16,0},{1,17},{17,1},{2,18},{18,2},{3,19},{19,3},{4,20},{20... | collective-permute-start | bytes 6291464 | tf_op jit(solution)/shard_map/ppermute | solution.py:99
  230.1 52.8 %collective-permute-start.23 = (bf16[2,256,1024]{2,1,0:T(8,128)(2,1)S(1)}, bf16[2,256,1024]{2,1,0:T(8,128)(2,1)S(1)}, u32[]{:S(2)}, u32[]{:S(2)}) collective-permute-start(bf16[2,256,1024]{2,1,0:T(8,128)(2,1)S(1)} %pad_maximum_fusion.19), channel_id=1, source_target_pairs={{0,4},{4,0},{1,5},{5,1},{2,6},{6,2},{3,7},{7,3},{8,12},{12,8},{9,1... | collective-permute-start | bytes 3145736 | tf_op jit(solution)/shard_map/ppermute | solution.py:50
  337.0 53.3 %collective-permute-start.28 = (bf16[512,1024]{1,0:T(8,128)(2,1)}, bf16[512,1024]{1,0:T(8,128)(2,1)}, u32[]{:S(2)}, u32[]{:S(2)}) collective-permute-start(bf16[512,1024]{1,0:T(8,128)(2,1)} %pad_maximum_fusion.20), channel_id=1, source_target_pairs={{0,4},{4,0},{1,5},{5,1},{2,6},{6,2},{3,7},{7,3},{8,12},{12,8},{9,1... | collective-permute-start | bytes 3145736 | tf_op jit(solution)/shard_map/ppermute | solution.py:50
  341.3 51.1 %collective-permute-start.29 = (bf16[512,1024]{1,0:T(8,128)(2,1)}, bf16[512,1024]{1,0:T(8,128)(2,1)}, u32[]{:S(2)}, u32[]{:S(2)}) collective-permute-start(bf16[512,1024]{1,0:T(8,128)(2,1)} %pad_maximum_fusion.21), channel_id=1, source_target_pairs={{0,8},{8,0},{1,9},{9,1},{2,10},{10,2},{3,11},{11,3},{4,12},{12,4},... | collective-permute-start | bytes 3145736 | tf_op jit(solution)/shard_map/ppermute | solution.py:50
  402.0 33.9 %collective-permute-start.30 = (bf16[1024,1024]{1,0:T(8,128)(2,1)S(1)}, bf16[1024,1024]{1,0:T(8,128)(2,1)S(1)}, u32[]{:S(2)}, u32[]{:S(2)}) collective-permute-start(bf16[1024,1024]{1,0:T(8,128)(2,1)S(1)} %add_convert_fusion.1), channel_id=1, source_target_pairs={{0,16},{16,0},{1,17},{17,1},{2,18},{18,2},{3,19},{19,3},{4,20},{20... | collective-permute-start | bytes 6291464 | tf_op jit(solution)/shard_map/ppermute | solution.py:99
  405.4 28.3 %collective-permute-start.33 = (bf16[256,1408]{1,0:T(8,128)(2,1)S(1)}, bf16[256,1408]{1,0:T(8,128)(2,1)S(1)}, u32[]{:S(2)}, u32[]{:S(2)}) collective-permute-start(bf16[256,1408]{1,0:T(8,128)(2,1)S(1)} %pad_maximum_fusion.28), channel_id=1, source_target_pairs={{0,4},{4,0},{1,5},{5,1},{2,6},{6,2},{3,7},{7,3},{8,12},{12,8},{9,1... | collective-permute-start | bytes 2162696 | tf_op jit(solution)/shard_map/ppermute | solution.py:50
  407.0 27.8 %collective-permute-start.34 = (bf16[256,1408]{1,0:T(8,128)(2,1)S(1)}, bf16[256,1408]{1,0:T(8,128)(2,1)S(1)}, u32[]{:S(2)}, u32[]{:S(2)}) collective-permute-start(bf16[256,1408]{1,0:T(8,128)(2,1)S(1)} %pad_maximum_fusion.29), channel_id=1, source_target_pairs={{0,8},{8,0},{1,9},{9,1},{2,10},{10,2},{3,11},{11,3},{4,12},{12,4},... | collective-permute-start | bytes 2162696 | tf_op jit(solution)/shard_map/ppermute | solution.py:50
  459.6 29.3 %collective-permute-start.35 = (bf16[1024,128]{1,0:T(8,128)(2,1)}, bf16[1024,128]{1,0:T(8,128)(2,1)}, u32[]{:S(2)}, u32[]{:S(2)}) collective-permute-start(bf16[1024,128]{1,0:T(8,128)(2,1)} %convolution_convert_fusion.6), channel_id=1, source_target_pairs={{4,0},{5,1},{6,2},{7,3},{12,8},{13,9},{14,10},{15,11},{20,16},{21,... | collective-permute-start | bytes 786440 | tf_op jit(solution)/shard_map/ppermute | solution.py:45
  467.4 74.1 %collective-permute-start.37 = (bf16[512,1024]{1,0:T(8,128)(2,1)}, bf16[512,1024]{1,0:T(8,128)(2,1)}, u32[]{:S(2)}, u32[]{:S(2)}) collective-permute-start(bf16[512,1024]{1,0:T(8,128)(2,1)} %pad_maximum_fusion.22), channel_id=1, source_target_pairs={{0,4},{4,0},{1,5},{5,1},{2,6},{6,2},{3,7},{7,3},{8,12},{12,8},{9,1... | collective-permute-start | bytes 3145736 | tf_op jit(solution)/shard_map/ppermute | solution.py:50
  472.3 70.8 %collective-permute-start.38 = (bf16[512,1024]{1,0:T(8,128)(2,1)}, bf16[512,1024]{1,0:T(8,128)(2,1)}, u32[]{:S(2)}, u32[]{:S(2)}) collective-permute-start(bf16[512,1024]{1,0:T(8,128)(2,1)} %pad_maximum_fusion.23), channel_id=1, source_target_pairs={{0,8},{8,0},{1,9},{9,1},{2,10},{10,2},{3,11},{11,3},{4,12},{12,4},... | collective-permute-start | bytes 3145736 | tf_op jit(solution)/shard_map/ppermute | solution.py:50
  474.1 73.4 %all-to-all-start.4 = ((bf16[4,256,512]{2,1,0:T(8,128)(2,1)}), bf16[4,256,512]{2,1,0:T(8,128)(2,1)}, u32[]{:S(2)}, u32[]{:S(2)}) async-start(bf16[4,256,512]{2,1,0:T(8,128)(2,1)} %maximum_maximum_fusion), calls=%async_computation.4 | async-start | bytes 2097152 | tf_op jit(solution)/shard_map/all_to_all | solution.py:79
  481.0 57.3 %collective-permute-start.39 = (bf16[128,1408]{1,0:T(8,128)(2,1)}, bf16[128,1408]{1,0:T(8,128)(2,1)}, u32[]{:S(2)}, u32[]{:S(2)}) collective-permute-start(bf16[128,1408]{1,0:T(8,128)(2,1)} %constant_dynamic-slice_fusion.24), channel_id=1, source_target_pairs={{0,8},{8,0},{1,9},{9,1},{2,10},{10,2},{3,11},{11,3},{4,12},{12,4},... | collective-permute-start | bytes 1081352 | tf_op jit(solution)/shard_map/ppermute | solution.py:50
  483.6 55.9 %collective-permute-start.40 = (bf16[128,1408]{1,0:T(8,128)(2,1)}, bf16[128,1408]{1,0:T(8,128)(2,1)}, u32[]{:S(2)}, u32[]{:S(2)}) collective-permute-start(bf16[128,1408]{1,0:T(8,128)(2,1)} %constant_dynamic-slice_fusion.23), channel_id=1, source_target_pairs={{0,4},{4,0},{1,5},{5,1},{2,6},{6,2},{3,7},{7,3},{8,12},{12,8},{9,1... | collective-permute-start | bytes 1081352 | tf_op jit(solution)/shard_map/ppermute | solution.py:50
  547.6 52.6 %all-to-all-start.3 = ((bf16[4,256,1024]{2,1,0:T(8,128)(2,1)}), bf16[4,256,1024]{2,1,0:T(8,128)(2,1)}, u32[]{:S(2)}, u32[]{:S(2)}) async-start(bf16[4,256,1024]{2,1,0:T(8,128)(2,1)} %bitcast.387), calls=%async_computation.3 | async-start | bytes 4194304 | tf_op jit(solution)/shard_map/all_to_all | solution.py:104
  562.5 24.2 %collective-permute-start.41 = (bf16[1024,1024]{1,0:T(8,128)(2,1)S(1)}, bf16[1024,1024]{1,0:T(8,128)(2,1)S(1)}, u32[]{:S(2)}, u32[]{:S(2)}) collective-permute-start(bf16[1024,1024]{1,0:T(8,128)(2,1)S(1)} %add_convert_fusion), channel_id=1, source_target_pairs={{0,16},{16,0},{1,17},{17,1},{2,18},{18,2},{3,19},{19,3},{4,20},{20... | collective-permute-start | bytes 6291464 | tf_op jit(solution)/shard_map/ppermute | solution.py:99
  600.1 28.7 %all-to-all-start.6 = ((bf16[4,256,512]{2,1,0:T(8,128)(2,1)}), bf16[4,256,512]{2,1,0:T(8,128)(2,1)S(1)}, u32[]{:S(2)}, u32[]{:S(2)}) async-start(bf16[4,256,512]{2,1,0:T(8,128)(2,1)} %bitcast.396), calls=%async_computation.6 | async-start | bytes 2097152 | tf_op jit(solution)/shard_map/all_to_all | solution.py:104
  607.5 25.1 %collective-permute-start.49 = (f32[2,8496]{1,0:T(2,128)}, f32[2,8496]{1,0:T(2,128)S(1)}, u32[]{:S(2)}, u32[]{:S(2)}) collective-permute-start(f32[2,8496]{1,0:T(2,128)} %pad_maximum_fusion.41), channel_id=1, source_target_pairs={{0,4},{4,0},{1,5},{5,1},{2,6},{6,2},{3,7},{7,3},{8,12},{12,8},{9,1... | collective-permute-start | bytes 203912 | tf_op jit(solution)/shard_map/ppermute | solution.py:50
  612.8 55.9 %collective-permute-start.47 = (bf16[256,1408]{1,0:T(8,128)(2,1)}, bf16[256,1408]{1,0:T(8,128)(2,1)}, u32[]{:S(2)}, u32[]{:S(2)}) collective-permute-start(bf16[256,1408]{1,0:T(8,128)(2,1)} %pad_maximum_fusion.31), channel_id=1, source_target_pairs={{0,8},{8,0},{1,9},{9,1},{2,10},{10,2},{3,11},{11,3},{4,12},{12,4},... | collective-permute-start | bytes 2162696 | tf_op jit(solution)/shard_map/ppermute | solution.py:50
  628.8 34.5 %all-to-all-start.8 = ((bf16[4,256,640]{2,1,0:T(8,128)(2,1)}), bf16[4,256,640]{2,1,0:T(8,128)(2,1)S(1)}, u32[]{:S(2)}, u32[]{:S(2)}) async-start(bf16[4,256,640]{2,1,0:T(8,128)(2,1)} %pad_maximum_fusion.15), calls=%async_computation.8 | async-start | bytes 2621440 | tf_op jit(solution)/shard_map/all_to_all | solution.py:79
  633.3 33.6 %collective-permute-start.50 = (f32[2,8496]{1,0:T(2,128)}, f32[2,8496]{1,0:T(2,128)}, u32[]{:S(2)}, u32[]{:S(2)}) collective-permute-start(f32[2,8496]{1,0:T(2,128)} %fusion.151), channel_id=1, source_target_pairs={{0,8},{8,0},{1,9},{9,1},{2,10},{10,2},{3,11},{11,3},{4,12},{12,4},... | collective-permute-start | bytes 203912 | tf_op jit(solution)/shard_map/ppermute | solution.py:50
  635.1 36.0 %collective-permute-start.45 = (bf16[256,1408]{1,0:T(8,128)(2,1)}, bf16[256,1408]{1,0:T(8,128)(2,1)}, u32[]{:S(2)}, u32[]{:S(2)}) collective-permute-start(bf16[256,1408]{1,0:T(8,128)(2,1)} %pad_maximum_fusion.30), channel_id=1, source_target_pairs={{0,4},{4,0},{1,5},{5,1},{2,6},{6,2},{3,7},{7,3},{8,12},{12,8},{9,1... | collective-permute-start | bytes 2162696 | tf_op jit(solution)/shard_map/ppermute | solution.py:50
  663.4 28.7 %all-to-all-start.5 = ((bf16[4,256,512]{2,1,0:T(8,128)(2,1)}), bf16[4,256,512]{2,1,0:T(8,128)(2,1)S(1)}, u32[]{:S(2)}, u32[]{:S(2)}) async-start(bf16[4,256,512]{2,1,0:T(8,128)(2,1)} %bitcast.397), calls=%async_computation.5 | async-start | bytes 2097152 | tf_op jit(solution)/shard_map/all_to_all | solution.py:104
  671.1 27.2 %collective-permute-start.48 = (bf16[128,1408]{1,0:T(8,128)(2,1)}, bf16[128,1408]{1,0:T(8,128)(2,1)}, u32[]{:S(2)}, u32[]{:S(2)}) collective-permute-start(bf16[128,1408]{1,0:T(8,128)(2,1)} %constant_dynamic-slice_fusion.10), channel_id=1, source_target_pairs={{0,4},{4,0},{1,5},{5,1},{2,6},{6,2},{3,7},{7,3},{8,12},{12,8},{9,1... | collective-permute-start | bytes 1081352 | tf_op jit(solution)/shard_map/ppermute | solution.py:50
  692.1 29.5 %all-to-all-start.9 = ((bf16[4,256,512]{2,1,0:T(8,128)(2,1)}), bf16[4,256,512]{2,1,0:T(8,128)(2,1)}, u32[]{:S(2)}, u32[]{:S(2)}) async-start(bf16[4,256,512]{2,1,0:T(8,128)(2,1)} %maximum_maximum_fusion.1), calls=%async_computation.9 | async-start | bytes 2097152 | tf_op jit(solution)/shard_map/all_to_all | solution.py:79
  721.6 38.7 %all-to-all-start.7 = ((bf16[4,288,640]{2,1,0:T(8,128)(2,1)}), bf16[4,288,640]{2,1,0:T(8,128)(2,1)}, u32[]{:S(2)}, u32[]{:S(2)}) async-start(bf16[4,288,640]{2,1,0:T(8,128)(2,1)} %pad_maximum_fusion.10), calls=%async_computation.7 | async-start | bytes 2949120 | tf_op jit(solution)/shard_map/all_to_all | solution.py:79
  733.1 35.1 %collective-permute-start.44 = (bf16[4,256,512]{2,1,0:T(8,128)(2,1)}, bf16[4,256,512]{2,1,0:T(8,128)(2,1)}, u32[]{:S(2)}, u32[]{:S(2)}) collective-permute-start(bf16[4,256,512]{2,1,0:T(8,128)(2,1)} %broadcast_select_fusion), channel_id=1, source_target_pairs={{0,16},{16,0},{1,17},{17,1},{2,18},{18,2},{3,19},{19,3},{4,20},{20... | collective-permute-start | bytes 3145736 | tf_op jit(solution)/shard_map/ppermute | solution.py:99
  (234 other events, 2421.4 us)

commit v2 on v1

--- a/solution.py
+++ b/solution.py
@@ -50,13 +50,15 @@
     return lax.ppermute(value, axis, [(i, (i + steps) % count) for i in range(count)])
 
 
-def line_gather(value, axis, dim=0):
+def line_gather(value, axis, dim=0, after=None):
     count = lax.axis_size(axis)
     place = lax.axis_index(axis)
     if count == 1:
         return jnp.expand_dims(value, dim)
     if count == 2:
         other = rotated(value, axis, 1)
+        if after is not None:
+            other, _ = tied(other, after)
         first = place == 0
         return jnp.stack([jnp.where(first, value, other), jnp.where(first, other, value)], axis=dim)
     up = down = value
@@ -79,12 +81,15 @@
     return jnp.sum(lax.all_to_all(blocks, "tp", 0, 0).astype(full), axis=0)
 
 
-def scatter_sum(pick, axis):
+def scatter_sum(pick, axis, after=None):
     count = lax.axis_size(axis)
     place = lax.axis_index(axis)
     total = pick(place).astype(full)
     for steps in range(1, count):
-        total = total + rotated(pick((place + steps) % count), axis, steps).astype(full)
+        arrived = rotated(pick((place + steps) % count), axis, steps)
+        if after is not None:
+            arrived, _ = tied(arrived, after)
+        total = total + arrived.astype(full)
     return total
 
 
@@ -104,10 +109,10 @@
     return lax.all_to_all(value.reshape(count, value.shape[0] // count, value.shape[1]), "tp", 0, 0)
 
 
-def gather_rows(early, late):
+def gather_rows(early, late, after):
     width = early.shape[-1]
-    half_a = line_gather(line_gather(early, "ctx"), "dp").reshape(-1, width)
-    half_b = line_gather(line_gather(late, "dp"), "ctx", 1).reshape(-1, width)
+    half_a = line_gather(line_gather(early, "ctx"), "dp", 0, after).reshape(-1, width)
+    half_b = line_gather(line_gather(late, "dp"), "ctx", 1, after).reshape(-1, width)
     return half_a, half_b
 
 
@@ -546,7 +551,7 @@
     return entering
 
 
-def layer_backward(incoming, valid, weights, params, kept, pending=None):
+def layer_backward(incoming, valid, weights, params, kept, beside, pending=None):
     gain, taps, step_bias, decay_log, skip, out_gain = params
     feed_weight, gate_weight, out_weight = weights
     (
@@ -579,7 +584,7 @@
     later = chain(local_adjoint, shrink, -1)
     early = whole_reduction(grad_gate, grad_out)
     if pending is not None:
-        back_ssm, feed.sums = tied(back_ssm, feed.sums)
+        back_ssm, (feed.sums, beside) = tied(back_ssm, (feed.sums, beside))
         feed.second()
     early.first()
     back_all, first_rows, sums, head_sums = ssm_backward(*scan, back_ssm, starts, later, *conv)
@@ -595,7 +600,8 @@
     if pending is not None:
         back_all, (pair.sums, feed.sums) = tied(back_all, (pair.sums, feed.sums))
         feed.sums = feed_sum(feed.sums, inner)
-    early.second()
+    else:
+        back_all, beside = tied(back_all, beside)
     grad_skip = jnp.sum(sums[CONV + 1, :inner].reshape(heads, HEADDIM), axis=1)
     grad_step_bias, grad_decay = head_sums[0, :heads], head_sums[1, :heads]
     grad_taps = sums[: CONV + 1]
@@ -612,14 +618,14 @@
             grad_out_gain, grad_step_bias, grad_decay, grad_skip, grad_gain,
         ]
     )
-    return delta, grad_feed, small, early
+    return delta, grad_feed, small, early, beside
 
 
 class Reduction:
     def __init__(self, half_a, half_b):
         self.half_a, self.half_b = half_a, half_b
 
-    def first(self):
+    def first(self, after=None):
         ndp, nctx = lax.axis_size("dp"), lax.axis_size("ctx")
 
         def rows_of(half, owners):
@@ -635,18 +641,18 @@
 
         self.sums = (
             scatter_sum(
-                lambda at: rows_of(self.half_a, [i * nctx + at for i in range(ndp)]), "ctx"
+                lambda at: rows_of(self.half_a, [i * nctx + at for i in range(ndp)]), "ctx", after
             ).astype(low),
             scatter_sum(
-                lambda at: rows_of(self.half_b, [at * nctx + j for j in range(nctx)]), "dp"
+                lambda at: rows_of(self.half_b, [at * nctx + j for j in range(nctx)]), "dp", after
             ).astype(low),
         )
 
-    def second(self):
+    def second(self, after=None):
         def own(value, axis):
             each = value.shape[0] // lax.axis_size(axis)
             return scatter_sum(
-                lambda at: lax.dynamic_slice_in_dim(value, at * each, each, 0), axis
+                lambda at: lax.dynamic_slice_in_dim(value, at * each, each, 0), axis, after
             ).astype(low)
 
         self.sums = own(self.sums[0], "dp"), own(self.sums[1], "ctx")
@@ -769,7 +775,7 @@
     cut = half + quarter + wide
     middle = tp_count // 2
 
-    def gather_item(part, sections):
+    def gather_item(part, sections, after=None):
         def side(pieces):
             parts, at = [], 0
             for size in sections:
@@ -777,7 +783,7 @@
                 at += size
             return columns(parts)
 
-        half_a, half_b = gather_rows(side(part[:middle]), side(part[middle:]))
+        half_a, half_b = gather_rows(side(part[:middle]), side(part[middle:]), after)
         result, at = [], 0
         for size in sections:
             result.append((half_a[:, at : at + middle * size], half_b[:, at : at + middle * size]))
@@ -804,20 +810,9 @@
     small_pad = jnp.pad(smalls[1], ((0, 0), (0, last_pack.shape[1] - cut)))
     along_last = tp_gather(jnp.concatenate([last_pack, small_pad], axis=0))
     pair_parts = gather_item(along_pair, pair_sections)
-    along_last, pair_parts = tied(along_last, pair_parts)
-    last_parts = gather_item(along_last[:, :own_rows, :cut], feed_sections)
-    along_last, last_parts = tied(along_last, last_parts)
-    last_parts += gather_item(along_last[:, :own_rows, cut:], pair_sections)
     feed_first, gain_first = feed_weights(feed_parts)
-    feed_last, gain_last = feed_weights(last_parts[:3])
-    weights = [
-        (feed_first, columns(pair_parts[0]), columns(pair_parts[1])),
-        (feed_last, columns(last_parts[3]), columns(last_parts[4])),
-    ]
-    params = [
-        (gain_first,) + layer_params(along_feed[:, own_rows:]),
-        (gain_last,) + layer_params(along_last[:, own_rows:, :cut]),
-    ]
+    weights = [(feed_first, columns(pair_parts[0]), columns(pair_parts[1]))]
+    params = [(gain_first,) + layer_params(along_feed[:, own_rows:])]
 
     places = lax.axis_index("ctx") * rows + jnp.arange(rows, dtype=jnp.int32)
     length = lax.dynamic_index_in_dim(lengths[:, 0], lane, 0, False)
@@ -828,6 +823,12 @@
     result_first, kept_first = layer_forward(hidden, before, valid, weights[0], params[0])
     low_first = result_first.astype(low)
     before = shifted(low_first[rows - RIM :], "ctx", 1)
+    last_parts = gather_item(along_last[:, :own_rows, :cut], feed_sections, low_first)
+    along_last, last_parts = tied(along_last, last_parts)
+    last_parts += gather_item(along_last[:, :own_rows, cut:], pair_sections)
+    feed_last, gain_last = feed_weights(last_parts[:3])
+    weights.append((feed_last, columns(last_parts[3]), columns(last_parts[4])))
+    params.append((gain_last,) + layer_params(along_last[:, own_rows:, :cut]))
     result_last, kept_last = layer_forward(low_first.astype(full), before, valid, weights[1], params[1])
     own_result = jnp.where(first, low_first, result_last.astype(low))
     quarter_rows = rows // tp_count
@@ -838,18 +839,20 @@
     def half_columns(value):
         return lax.dynamic_slice_in_dim(value.astype(low), column, width // 2, 1)
 
-    delta_last, feed_last, small_last, pair_last = layer_backward(
-        out_grad, valid, weights[1], params[1], kept_last
-    )
-    last = split_reduction(feed_last)
-    last.first()
+    delta_last, feed_last, small_last, pair_last, section_out = layer_backward(
+        out_grad, valid, weights[1], params[1], kept_last, section_out
+    )
     spread_last = spread_rows(half_columns(delta_last))
     incoming = (out_grad + delta_last).astype(low).astype(full)
-    delta_first, feed_first, small_first, pair_first = layer_backward(
-        incoming, valid, weights[0], params[0], kept_first, (pair_last, last)
+    pair_last.second(incoming)
+    last = split_reduction(feed_last)
+    last.first(incoming)
+    delta_first, feed_first, small_first, pair_first, spread_last = layer_backward(
+        incoming, valid, weights[0], params[0], kept_first, spread_last, (pair_last, last)
     )
     grad_first = (incoming + delta_first).astype(low)
-    feed_first, (grad_first, pair_first.sums) = tied(feed_first, (grad_first, pair_first.sums))
+    pair_first.second(grad_first)
+    feed_first, grad_first = tied(feed_first, grad_first)
     feed = split_reduction(feed_first)
     feed.first()
     pair_first_sum = pair_sum(pair_first.sums)

time: 807 us -> 777 us (0.963)
  waiting for transfers between devices: 232 us -> 187 us
  matrix products: 86.7 us -> 102 us
    all_to_all x3, waiting for transfers between devices: 44.6 us -> 15 us  [spread_rows(): lax.all_to_all(value.reshape(count, value.shape[0] // count, value.shape[...]
    all_to_all x4, waiting for transfers between devices: 64.6 us -> 40.2 us  [tp_sum(): return jnp.sum(lax.all_to_all(blocks, 'tp', 0, 0).astype(full), axis=0)]
    all_to_all x3, waiting for transfers between devices: 15.4 us -> 38.5 us  [tp_gather(): return lax.all_to_all(copies, 'tp', 0, 0)]
    ppermute x8, waiting for transfers between devices: 18.8 us -> 10.6 us  [shifted(): lax.ppermute(value, axis, [(source, source + steps) for source in range(f...]
    unnamed x441 -> x455, local copies, waits for them, and re-layouts: 42.5 us -> 38.1 us
  transfers between devices with their start and end apart: 63 -> 63, of which waited for: 27 -> 27; matrix products, arithmetic and copies ran while one was open for 27% -> 31% of each run, Pallas kernels for 14% -> 15%
where the time goes in v2:
time: 777 us; the launch traced here: 768 us
  waiting for transfers between devices  187 us (24%)
  other arithmetic  145 us (19%)
  Pallas kernels  113 us (15%)
  starting transfers between devices  110 us (14%)
  local copies, waits for them, and re-layouts  106 us (14%)
  matrix products  102 us (13%)
    ppermute x34, waiting for transfers between devices, rotated(): lax.ppermute(value, axis, [(i, (i + steps) % count) for i in range(count)])  80.7 us
    pallas_call x2, Pallas kernels, ssm_backward(): pl.pallas_call(bwd_kernel, grid=(blocks,), in_specs=[pl.BlockSpec((CHUNK,...  69.1 us
    dot_general x10, matrix products, dot_nn(): lax.dot_general(a, b, (((1,), (0,)), ((), ())), precision=precision, pref...  44.3 us
    all_to_all x4, waiting for transfers between devices, tp_sum(): return jnp.sum(lax.all_to_all(blocks, 'tp', 0, 0).astype(full), axis=0)  40.2 us
    all_to_all x3, waiting for transfers between devices, tp_gather(): return lax.all_to_all(copies, 'tp', 0, 0)  38.5 us
    unnamed x455, local copies, waits for them, and re-layouts  38.1 us
    dot_general x8, matrix products, dot_tn(): lax.dot_general(a, b, (((0,), (0,)), ((), ())), precision=precision, pref...  31.2 us
    ppermute x34, starting transfers between devices, rotated(): lax.ppermute(value, axis, [(i, (i + steps) % count) for i in range(count)])  30.4 us
  transfers between devices with their start and end apart: 63, of which 27 were waited for; matrix products, arithmetic and copies ran while one was open for 31% of the time, Pallas kernels for 15%

profile of v2, /device:TPU:1, one launch (start us, length us, event | category | flops | bytes accessed | tf_op | source)
XLA Modules:
  0.0 768.2 jit_solution(777318507168123751)
XLA Ops:
  9.3 5.9 all-to-all-start
  22.1 15.0 %all-to-all-done = bf16[4,288,384]{2,1,0:T(8,128)(2,1)S(1)} async-done(((bf16[4,288,384]{2,1,0:T(8,128)(2,1)}), bf16[4,288,384]{2,1,0:T(8,128)(2,1)S(1)}, u32[]{:S(2)}, u32[]{:S(2)}) %all-to-all-start) | async-done | bytes 884768 | tf_op jit(solution)/shard_map/all_to_all | solution.py:77
  40.6 6.4 collective-permute-done.2
  56.8 8.3 %collective-permute-done.3 = bf16[2,256,768]{2,1,0:T(8,128)(2,1)} collective-permute-done((bf16[2,256,768]{2,1,0:T(8,128)(2,1)}, bf16[2,256,768]{2,1,0:T(8,128)(2,1)}, u32[]{:S(2)}, u32[]{:S(2)}) %collective-permute-start.3) | collective-permute-done | bytes 786464 | tf_op jit(solution)/shard_map/ppermute | solution.py:50
  70.1 11.8 %all-to-all-done.1 = bf16[4,256,512]{2,1,0:T(8,128)(2,1)S(1)} async-done(((bf16[4,256,512]{2,1,0:T(8,128)(2,1)}), bf16[4,256,512]{2,1,0:T(8,128)(2,1)S(1)}, u32[]{:S(2)}, u32[]{:S(2)}) %all-to-all-start.1) | async-done | bytes 1048608 | tf_op jit(solution)/shard_map/all_to_all | solution.py:77
  86.7 6.1 fusion.166
  101.9 9.7 %mixer_prep.2 = (f32[1024,1280]{1,0:T(8,128)S(1)}, f32[1024,128]{1,0:T(8,128)S(1)}, f32[1024,128]{1,0:T(8,128)S(1)}, f32[16,1024]{1,0:T(8,128)S(1)}, f32[1024,128]{1,0:T(8,128)S(1)}, /*index=5*/f32[1024,128]{1,0:T(8,128)S(1)}) custom-call(bf16[1024,1280]{1,0:T(8,128)(2,1)S(1)} %slice.1039.feed_ref.before_ref, bf16[16,1280]{1,0:T(8,128)(2,1)S(1)} %fusion.50.rim_ref, ...), custom_call_target="tpu_custom_call" | custom-call | flops 268435456 | bytes 7864320 | tf_op jit(solution)/shard_map/mixer_prep/pallas_call | solution.py:188
  127.8 12.2 %ssm_forward.2 = (f32[1024,1024]{1,0:T(8,128)S(1)}, bf16[8,1024,128]{2,1,0:T(8,128)(2,1)S(1)}) custom-call(f32[1024,1280]{1,0:T(8,128)S(1)} %copy-done.3, f32[1024,1280]{1,0:T(8,128)S(1)} %copy-done.3, f32[1024,128]{1,0:T(8,128)S(1)} %get-tuple-element.94.dt_ref, f32[1024,128]{1,0:T(8,128)S(1)} %get-tuple-element.95.cum_ref, ...), custom_call_target="tpu_custom_call" | custom-call | flops 1073741824 | bytes 10485760 | tf_op jit(solution)/shard_map/ssm_forward/pallas_call | solution.py:394
  145.6 7.9 %multiply_reduce_fusion.3 = (f32[1024]{0:T(1024)S(1)}, f32[1024,1024]{1,0:T(8,128)S(1)}, f32[1024,1024]{1,0:T(8,128)}) fusion(f32[1024,1024]{1,0:T(8,128)S(1)} %get-tuple-element.98, bf16[1024,512]{1,0:T(8,128)(2,1)S(1)} %get-tuple-element.273, bf16[1024,512]{1,0:T(8,128)(2,1)S(1)} %get-tuple-element.271, f32[1024]{0:T(1024)S(1)} %convert_reduce_fusion.5, ...), kind=kOutput, calls=%fused_computation.65 | convolution fusion | flops 2163211264 | bytes 16789508 | tf_op jit(solution)/shard_map/dot_general | solution.py:25
  160.5 11.7 %all-to-all-done.2 = bf16[4,288,896]{2,1,0:T(8,128)(2,1)S(1)} async-done(((bf16[4,288,896]{2,1,0:T(8,128)(2,1)}), bf16[4,288,896]{2,1,0:T(8,128)(2,1)S(1)}, u32[]{:S(2)}, u32[]{:S(2)}) %all-to-all-start.2) | async-done | bytes 2064416 | tf_op jit(solution)/shard_map/all_to_all | solution.py:77
  193.9 8.8 %collective-permute-done.15 = bf16[2,256,768]{2,1,0:T(8,128)(2,1)S(1)} collective-permute-done((bf16[2,256,768]{2,1,0:T(8,128)(2,1)S(1)}, bf16[2,256,768]{2,1,0:T(8,128)(2,1)S(1)}, u32[]{:S(2)}, u32[]{:S(2)}) %collective-permute-start.15) | collective-permute-done | bytes 786464 | tf_op jit(solution)/shard_map/ppermute | solution.py:50
  253.3 9.7 %mixer_prep.3 = (f32[1024,1280]{1,0:T(8,128)S(1)}, f32[1024,128]{1,0:T(8,128)S(1)}, f32[1024,128]{1,0:T(8,128)S(1)}, f32[16,1024]{1,0:T(8,128)S(1)}, f32[1024,128]{1,0:T(8,128)S(1)}, /*index=5*/f32[1024,128]{1,0:T(8,128)S(1)}) custom-call(bf16[1024,1280]{1,0:T(8,128)(2,1)S(1)} %slice.1038.feed_ref.before_ref, bf16[16,1280]{1,0:T(8,128)(2,1)S(1)} %fusion.47.rim_ref, ...), custom_call_target="tpu_custom_call" | custom-call | flops 268435456 | bytes 7864320 | tf_op jit(solution)/shard_map/mixer_prep/pallas_call | solution.py:188
  287.9 12.2 %ssm_forward.3 = (f32[1024,1024]{1,0:T(8,128)S(1)}, bf16[8,1024,128]{2,1,0:T(8,128)(2,1)S(1)}) custom-call(f32[1024,1280]{1,0:T(8,128)S(1)} %copy-done.5, f32[1024,1280]{1,0:T(8,128)S(1)} %copy-done.5, f32[1024,128]{1,0:T(8,128)S(1)} %copy-done.23, f32[1024,128]{1,0:T(8,128)S(1)} %copy-done.26, f32[16,1024]{1,0:T(8,128)S(1)} %get-tuple-element.113.cumt_ref, ...), custom_call_target="tpu_custom_call" | custom-call | flops 1073741824 | bytes 10485760 | tf_op jit(solution)/shard_map/ssm_forward/pallas_call | solution.py:394
  308.1 5.8 multiply_reduce_fusion.2
  348.7 8.3 %multiply_convert_fusion.3 = (bf16[1024,1024]{1,0:T(8,128)(2,1)S(1)}, f32[1024,1024]{1,0:T(8,128)S(1)}, f32[1024]{0:T(1024)}) fusion(f32[1024,1024]{1,0:T(8,128)} %get-tuple-element.447, f32[1024,1024]{1,0:T(8,128)S(1)} %copy-done.55, f32[1024,1024]{1,0:T(8,128)} %copy-done.207, f32[1024]{0:T(1024)} %fusion.126, f32[1024]{0:T(1024)} %bitcast.407, ...), kind=kOutput, calls=%fused_computation.55 | convolution fusion | flops 2171599872 | bytes 23085056 | tf_op jit(solution)/shard_map/dot_general | solution.py:25
  365.5 5.2 collective-permute-done.26.later_ref
  370.7 34.5 %ssm_backward.2 = (bf16[1024,1408]{1,0:T(8,128)(2,1)}, f32[8,1280]{1,0:T(8,128)S(1)}, f32[8,1280]{1,0:T(8,128)S(1)}, f32[8,128]{1,0:T(8,128)S(1)}) custom-call(f32[1024,1280]{1,0:T(8,128)} %copy-done.4, f32[1024,1280]{1,0:T(8,128)} %copy-done.4, f32[1024,128]{1,0:T(8,128)S(1)} %copy-done.24, f32[1024,128]{1,0:T(8,128)S(1)} %copy-done.27, ...), custom_call_target="tpu_custom_call" | custom-call | flops 4294967296 | bytes 16777216 | tf_op jit(solution)/shard_map/ssm_backward/pallas_call | solution.py:437
  411.9 19.8 %collective-permute-done.28 = bf16[512,1024]{1,0:T(8,128)(2,1)S(1)} collective-permute-done((bf16[512,1024]{1,0:T(8,128)(2,1)S(1)}, bf16[512,1024]{1,0:T(8,128)(2,1)S(1)}, u32[]{:S(2)}, u32[]{:S(2)}) %collective-permute-start.28) | collective-permute-done | bytes 1048608 | tf_op jit(solution)/shard_map/ppermute | solution.py:50
  433.1 6.3 fusion.188
  450.8 6.1 convolution_convert_fusion.1
  465.7 7.7 %fusion.2 = (f32[1024]{0:T(1024)S(1)}, bf16[1024,1024]{1,0:T(8,128)(2,1)S(1)}, f32[1024,1024]{1,0:T(8,128)}, bf16[1024,1024]{1,0:T(8,128)(2,1)}) fusion(bf16[1024,1024]{1,0:T(8,128)(2,1)} %collective-permute-done.13, bf16[1024,1024]{1,0:T(8,128)(2,1)} %convolution_convert_fusion.5, f32[1024]{0:T(1024)S(1)} %copy-done.174, f32[4,1,1024,1024]{3,2,1,0:T(8,128)} %param.15, ...), kind=kLoop, calls=%fused_computation.21 | loop fusion | flops 23067648 | bytes 23089156 | tf_op jit(solution)/shard_map/reduce_sum | solution.py:573
  479.3 6.7 fusion.71
  497.3 5.4 multiply_convert_fusion
  530.4 8.6 %collective-permute-done.37 = bf16[512,1024]{1,0:T(8,128)(2,1)} collective-permute-done((bf16[512,1024]{1,0:T(8,128)(2,1)}, bf16[512,1024]{1,0:T(8,128)(2,1)}, u32[]{:S(2)}, u32[]{:S(2)}) %collective-permute-start.37) | collective-permute-done | bytes 1048608 | tf_op jit(solution)/shard_map/ppermute | solution.py:50
  542.0 34.6 %ssm_backward.3 = (bf16[1024,1408]{1,0:T(8,128)(2,1)S(1)}, f32[8,1280]{1,0:T(8,128)S(1)}, f32[8,1280]{1,0:T(8,128)S(1)}, f32[8,128]{1,0:T(8,128)S(1)}) custom-call(f32[1024,1280]{1,0:T(8,128)} %copy-done.2, f32[1024,1280]{1,0:T(8,128)} %copy-done.2, f32[1024,128]{1,0:T(8,128)S(1)} %copy-done.19, f32[1024,128]{1,0:T(8,128)S(1)} %copy-done.21, ...), custom_call_target="tpu_custom_call" | custom-call | flops 4294967296 | bytes 16777216 | tf_op jit(solution)/shard_map/ssm_backward/pallas_call | solution.py:437
  589.6 5.4 fusion.189
  611.5 6.9 convolution_convert_fusion
  656.2 15.0 %all-to-all-done.6 = bf16[4,256,512]{2,1,0:T(8,128)(2,1)S(1)} async-done(((bf16[4,256,512]{2,1,0:T(8,128)(2,1)}), bf16[4,256,512]{2,1,0:T(8,128)(2,1)S(1)}, u32[]{:S(2)}, u32[]{:S(2)}) %all-to-all-start.6) | async-done | bytes 1048608 | tf_op jit(solution)/shard_map/all_to_all | solution.py:109
  677.4 6.0 collective-permute-done.46
  684.9 15.1 %all-to-all-done.9 = bf16[4,256,512]{2,1,0:T(8,128)(2,1)S(1)} async-done(((bf16[4,256,512]{2,1,0:T(8,128)(2,1)}), bf16[4,256,512]{2,1,0:T(8,128)(2,1)S(1)}, u32[]{:S(2)}, u32[]{:S(2)}) %all-to-all-start.9) | async-done | bytes 1048608 | tf_op jit(solution)/shard_map/all_to_all | solution.py:81
  718.3 20.8 %all-to-all-done.7 = bf16[4,288,640]{2,1,0:T(8,128)(2,1)S(1)} async-done(((bf16[4,288,640]{2,1,0:T(8,128)(2,1)}), bf16[4,288,640]{2,1,0:T(8,128)(2,1)S(1)}, u32[]{:S(2)}, u32[]{:S(2)}) %all-to-all-start.7) | async-done | bytes 1474592 | tf_op jit(solution)/shard_map/all_to_all | solution.py:81
  744.8 5.3 add_select_fusion
  (912 shorter events, 414.1 us)
Async XLA Ops:
  9.3 27.8 %all-to-all-start = ((bf16[4,288,384]{2,1,0:T(8,128)(2,1)}), bf16[4,288,384]{2,1,0:T(8,128)(2,1)S(1)}, u32[]{:S(2)}, u32[]{:S(2)}) async-start(bf16[4,288,384]{2,1,0:T(8,128)(2,1)} %broadcast_in_dim.38), calls=%async_computation | async-start | bytes 1769472 | tf_op jit(solution)/shard_map/all_to_all | solution.py:77
  53.1 28.9 %all-to-all-start.1 = ((bf16[4,256,512]{2,1,0:T(8,128)(2,1)}), bf16[4,256,512]{2,1,0:T(8,128)(2,1)S(1)}, u32[]{:S(2)}, u32[]{:S(2)}) async-start(bf16[4,256,512]{2,1,0:T(8,128)(2,1)} %broadcast_in_dim.78), calls=%async_computation.1 | async-start | bytes 2097152 | tf_op jit(solution)/shard_map/all_to_all | solution.py:77
  98.7 41.3 %collective-permute-start.11 = (bf16[2,256,1024]{2,1,0:T(8,128)(2,1)}, bf16[2,256,1024]{2,1,0:T(8,128)(2,1)}, u32[]{:S(2)}, u32[]{:S(2)}) collective-permute-start(bf16[2,256,1024]{2,1,0:T(8,128)(2,1)} %pad_maximum_fusion.23), channel_id=1, source_target_pairs={{0,4},{4,0},{1,5},{5,1},{2,6},{6,2},{3,7},{7,3},{8,12},{12,8},{9,1... | collective-permute-start | bytes 3145736 | tf_op jit(solution)/shard_map/ppermute | solution.py:50
  100.4 42.2 %collective-permute-start.9 = (bf16[2,256,1024]{2,1,0:T(8,128)(2,1)}, bf16[2,256,1024]{2,1,0:T(8,128)(2,1)}, u32[]{:S(2)}, u32[]{:S(2)}) collective-permute-start(bf16[2,256,1024]{2,1,0:T(8,128)(2,1)} %pad_maximum_fusion.22), channel_id=1, source_target_pairs={{0,8},{8,0},{1,9},{9,1},{2,10},{10,2},{3,11},{11,3},{4,12},{12,4},... | collective-permute-start | bytes 3145736 | tf_op jit(solution)/shard_map/ppermute | solution.py:50
  121.4 50.8 %all-to-all-start.2 = ((bf16[4,288,896]{2,1,0:T(8,128)(2,1)}), bf16[4,288,896]{2,1,0:T(8,128)(2,1)S(1)}, u32[]{:S(2)}, u32[]{:S(2)}) async-start(bf16[4,288,896]{2,1,0:T(8,128)(2,1)} %broadcast_in_dim.80), calls=%async_computation.2 | async-start | bytes 4128768 | tf_op jit(solution)/shard_map/all_to_all | solution.py:77
  157.3 31.8 %collective-permute-start.13 = (bf16[1024,1024]{1,0:T(8,128)(2,1)}, bf16[1024,1024]{1,0:T(8,128)(2,1)}, u32[]{:S(2)}, u32[]{:S(2)}) collective-permute-start(bf16[1024,1024]{1,0:T(8,128)(2,1)} %convolution_convert_fusion.5), channel_id=1, source_target_pairs={{0,16},{16,0},{1,17},{17,1},{2,18},{18,2},{3,19},{19,3},{4,20},{20... | collective-permute-start | bytes 6291464 | tf_op jit(solution)/shard_map/ppermute | solution.py:104
  183.7 19.0 %collective-permute-start.15 = (bf16[2,256,768]{2,1,0:T(8,128)(2,1)S(1)}, bf16[2,256,768]{2,1,0:T(8,128)(2,1)S(1)}, u32[]{:S(2)}, u32[]{:S(2)}) collective-permute-start(bf16[2,256,768]{2,1,0:T(8,128)(2,1)S(1)} %pad_maximum_fusion.32), channel_id=1, source_target_pairs={{0,8},{8,0},{1,9},{9,1},{2,10},{10,2},{3,11},{11,3},{4,12},{12,4},... | collective-permute-start | bytes 2359304 | tf_op jit(solution)/shard_map/ppermute | solution.py:50
  221.7 23.7 %collective-permute-start.18 = (bf16[16,1024]{1,0:T(8,128)(2,1)}, bf16[16,1024]{1,0:T(8,128)(2,1)}, u32[]{:S(2)}, u32[]{:S(2)}) collective-permute-start(bf16[16,1024]{1,0:T(8,128)(2,1)} %slice.817), channel_id=1, source_target_pairs={{0,4},{1,5},{2,6},{3,7},{8,12},{9,13},{10,14},{11,15},{16,20},{17,... | collective-permute-start | bytes 98312 | tf_op jit(solution)/shard_map/ppermute | solution.py:45
  245.3 26.5 %collective-permute-start.20 = (bf16[256,1024]{1,0:T(8,128)(2,1)}, bf16[256,1024]{1,0:T(8,128)(2,1)S(1)}, u32[]{:S(2)}, u32[]{:S(2)}) collective-permute-start(bf16[256,1024]{1,0:T(8,128)(2,1)} %pad_maximum_fusion.42), channel_id=1, source_target_pairs={{0,4},{4,0},{1,5},{5,1},{2,6},{6,2},{3,7},{7,3},{8,12},{12,8},{9,1... | collective-permute-start | bytes 1572872 | tf_op jit(solution)/shard_map/ppermute | solution.py:50
  251.5 48.6 %collective-permute-start.23 = (bf16[2,256,1024]{2,1,0:T(8,128)(2,1)}, bf16[2,256,1024]{2,1,0:T(8,128)(2,1)}, u32[]{:S(2)}, u32[]{:S(2)}) collective-permute-start(bf16[2,256,1024]{2,1,0:T(8,128)(2,1)} %pad_maximum_fusion.25), channel_id=1, source_target_pairs={{0,4},{4,0},{1,5},{5,1},{2,6},{6,2},{3,7},{7,3},{8,12},{12,8},{9,1... | collective-permute-start | bytes 3145736 | tf_op jit(solution)/shard_map/ppermute | solution.py:50
  273.9 29.0 %collective-permute-start.21 = (bf16[2,256,1024]{2,1,0:T(8,128)(2,1)}, bf16[2,256,1024]{2,1,0:T(8,128)(2,1)}, u32[]{:S(2)}, u32[]{:S(2)}) collective-permute-start(bf16[2,256,1024]{2,1,0:T(8,128)(2,1)} %pad_maximum_fusion.24), channel_id=1, source_target_pairs={{0,8},{8,0},{1,9},{9,1},{2,10},{10,2},{3,11},{11,3},{4,12},{12,4},... | collective-permute-start | bytes 3145736 | tf_op jit(solution)/shard_map/ppermute | solution.py:50
  340.8 92.4 %all-to-all-start.3 = ((bf16[4,256,1024]{2,1,0:T(8,128)(2,1)}), bf16[4,256,1024]{2,1,0:T(8,128)(2,1)}, u32[]{:S(2)}, u32[]{:S(2)}) async-start(bf16[4,256,1024]{2,1,0:T(8,128)(2,1)} %bitcast.384), calls=%async_computation.3 | async-start | bytes 4194304 | tf_op jit(solution)/shard_map/all_to_all | solution.py:109
  347.2 64.3 %collective-permute-start.29 = (bf16[512,1024]{1,0:T(8,128)(2,1)S(1)}, bf16[512,1024]{1,0:T(8,128)(2,1)S(1)}, u32[]{:S(2)}, u32[]{:S(2)}) collective-permute-start(bf16[512,1024]{1,0:T(8,128)(2,1)S(1)} %pad_maximum_fusion.27), channel_id=1, source_target_pairs={{0,8},{8,0},{1,9},{9,1},{2,10},{10,2},{3,11},{11,3},{4,12},{12,4},... | collective-permute-start | bytes 3145736 | tf_op jit(solution)/shard_map/ppermute | solution.py:50
  406.6 25.1 %collective-permute-start.28 = (bf16[512,1024]{1,0:T(8,128)(2,1)S(1)}, bf16[512,1024]{1,0:T(8,128)(2,1)S(1)}, u32[]{:S(2)}, u32[]{:S(2)}) collective-permute-start(bf16[512,1024]{1,0:T(8,128)(2,1)S(1)} %pad_maximum_fusion.26), channel_id=1, source_target_pairs={{0,4},{4,0},{1,5},{5,1},{2,6},{6,2},{3,7},{7,3},{8,12},{12,8},{9,1... | collective-permute-start | bytes 3145736 | tf_op jit(solution)/shard_map/ppermute | solution.py:50
  443.2 18.6 %collective-permute-start.30 = (bf16[1024,1024]{1,0:T(8,128)(2,1)}, bf16[1024,1024]{1,0:T(8,128)(2,1)}, u32[]{:S(2)}, u32[]{:S(2)}) collective-permute-start(bf16[1024,1024]{1,0:T(8,128)(2,1)} %add_convert_fusion.1), channel_id=1, source_target_pairs={{0,16},{16,0},{1,17},{17,1},{2,18},{18,2},{3,19},{19,3},{4,20},{20... | collective-permute-start | bytes 6291464 | tf_op jit(solution)/shard_map/ppermute | solution.py:104
  447.6 31.7 %collective-permute-start.32 = (bf16[256,1024]{1,0:T(8,128)(2,1)}, bf16[256,1024]{1,0:T(8,128)(2,1)}, u32[]{:S(2)}, u32[]{:S(2)}) collective-permute-start(bf16[256,1024]{1,0:T(8,128)(2,1)} %constant_dynamic-slice_fusion.41), channel_id=1, source_target_pairs={{0,4},{4,0},{1,5},{5,1},{2,6},{6,2},{3,7},{7,3},{8,12},{12,8},{9,1... | collective-permute-start | bytes 1572872 | tf_op jit(solution)/shard_map/ppermute | solution.py:50
  450.3 35.7 %collective-permute-start.31 = (bf16[256,1024]{1,0:T(8,128)(2,1)}, bf16[256,1024]{1,0:T(8,128)(2,1)}, u32[]{:S(2)}, u32[]{:S(2)}) collective-permute-start(bf16[256,1024]{1,0:T(8,128)(2,1)} %constant_dynamic-slice_fusion.42), channel_id=1, source_target_pairs={{0,8},{8,0},{1,9},{9,1},{2,10},{10,2},{3,11},{11,3},{4,12},{12,4},... | collective-permute-start | bytes 1572872 | tf_op jit(solution)/shard_map/ppermute | solution.py:50
  459.2 20.1 %collective-permute-start.33 = (bf16[256,1408]{1,0:T(8,128)(2,1)}, bf16[256,1408]{1,0:T(8,128)(2,1)}, u32[]{:S(2)}, u32[]{:S(2)}) collective-permute-start(bf16[256,1408]{1,0:T(8,128)(2,1)} %pad_maximum_fusion.34), channel_id=1, source_target_pairs={{0,4},{4,0},{1,5},{5,1},{2,6},{6,2},{3,7},{7,3},{8,12},{12,8},{9,1... | collective-permute-start | bytes 2162696 | tf_op jit(solution)/shard_map/ppermute | solution.py:50
  487.1 33.7 %all-to-all-start.4 = ((bf16[4,256,512]{2,1,0:T(8,128)(2,1)}), bf16[4,256,512]{2,1,0:T(8,128)(2,1)}, u32[]{:S(2)}, u32[]{:S(2)}) async-start(bf16[4,256,512]{2,1,0:T(8,128)(2,1)} %bitcast.116), calls=%async_computation.4 | async-start | bytes 2097152 | tf_op jit(solution)/shard_map/all_to_all | solution.py:109
  497.1 30.2 %collective-permute-start.38 = (bf16[512,1024]{1,0:T(8,128)(2,1)}, bf16[512,1024]{1,0:T(8,128)(2,1)}, u32[]{:S(2)}, u32[]{:S(2)}) collective-permute-start(bf16[512,1024]{1,0:T(8,128)(2,1)} %pad_maximum_fusion.29), channel_id=1, source_target_pairs={{0,8},{8,0},{1,9},{9,1},{2,10},{10,2},{3,11},{11,3},{4,12},{12,4},... | collective-permute-start | bytes 3145736 | tf_op jit(solution)/shard_map/ppermute | solution.py:50
  507.4 34.5 %collective-permute-start.35 = (bf16[1024,128]{1,0:T(8,128)(2,1)}, bf16[1024,128]{1,0:T(8,128)(2,1)S(1)}, u32[]{:S(2)}, u32[]{:S(2)}) collective-permute-start(bf16[1024,128]{1,0:T(8,128)(2,1)} %convolution_convert_fusion.6), channel_id=1, source_target_pairs={{4,0},{5,1},{6,2},{7,3},{12,8},{13,9},{14,10},{15,11},{20,16},{21,... | collective-permute-start | bytes 786440 | tf_op jit(solution)/shard_map/ppermute | solution.py:45
  515.3 23.7 %collective-permute-start.37 = (bf16[512,1024]{1,0:T(8,128)(2,1)}, bf16[512,1024]{1,0:T(8,128)(2,1)}, u32[]{:S(2)}, u32[]{:S(2)}) collective-permute-start(bf16[512,1024]{1,0:T(8,128)(2,1)} %pad_maximum_fusion.28), channel_id=1, source_target_pairs={{0,4},{4,0},{1,5},{5,1},{2,6},{6,2},{3,7},{7,3},{8,12},{12,8},{9,1... | collective-permute-start | bytes 3145736 | tf_op jit(solution)/shard_map/ppermute | solution.py:50
  520.7 61.7 %all-to-all-start.5 = ((bf16[4,256,512]{2,1,0:T(8,128)(2,1)}), bf16[4,256,512]{2,1,0:T(8,128)(2,1)}, u32[]{:S(2)}, u32[]{:S(2)}) async-start(bf16[4,256,512]{2,1,0:T(8,128)(2,1)} %maximum_maximum_fusion), calls=%async_computation.5 | async-start | bytes 2097152 | tf_op jit(solution)/shard_map/all_to_all | solution.py:81
  598.8 19.7 %collective-permute-start.41 = (bf16[1024,1024]{1,0:T(8,128)(2,1)}, bf16[1024,1024]{1,0:T(8,128)(2,1)}, u32[]{:S(2)}, u32[]{:S(2)}) collective-permute-start(bf16[1024,1024]{1,0:T(8,128)(2,1)} %add_convert_fusion), channel_id=1, source_target_pairs={{0,16},{16,0},{1,17},{17,1},{2,18},{18,2},{3,19},{19,3},{4,20},{20... | collective-permute-start | bytes 6291464 | tf_op jit(solution)/shard_map/ppermute | solution.py:104
  603.4 23.6 %collective-permute-start.50 = (bf16[256,1024]{1,0:T(8,128)(2,1)}, bf16[256,1024]{1,0:T(8,128)(2,1)}, u32[]{:S(2)}, u32[]{:S(2)}) collective-permute-start(bf16[256,1024]{1,0:T(8,128)(2,1)} %constant_dynamic-slice_fusion.10), channel_id=1, source_target_pairs={{0,4},{4,0},{1,5},{5,1},{2,6},{6,2},{3,7},{7,3},{8,12},{12,8},{9,1... | collective-permute-start | bytes 1572872 | tf_op jit(solution)/shard_map/ppermute | solution.py:50
  604.4 24.2 %collective-permute-start.49 = (bf16[256,1024]{1,0:T(8,128)(2,1)}, bf16[256,1024]{1,0:T(8,128)(2,1)}, u32[]{:S(2)}, u32[]{:S(2)}) collective-permute-start(bf16[256,1024]{1,0:T(8,128)(2,1)} %constant_dynamic-slice_fusion.11), channel_id=1, source_target_pairs={{0,8},{8,0},{1,9},{9,1},{2,10},{10,2},{3,11},{11,3},{4,12},{12,4},... | collective-permute-start | bytes 1572872 | tf_op jit(solution)/shard_map/ppermute | solution.py:50
  607.0 35.6 %all-to-all-start.8 = ((bf16[4,256,640]{2,1,0:T(8,128)(2,1)}), bf16[4,256,640]{2,1,0:T(8,128)(2,1)}, u32[]{:S(2)}, u32[]{:S(2)}) async-start(bf16[4,256,640]{2,1,0:T(8,128)(2,1)} %pad_maximum_fusion.21), calls=%async_computation.8 | async-start | bytes 2621440 | tf_op jit(solution)/shard_map/all_to_all | solution.py:81
  642.6 28.7 %all-to-all-start.6 = ((bf16[4,256,512]{2,1,0:T(8,128)(2,1)}), bf16[4,256,512]{2,1,0:T(8,128)(2,1)S(1)}, u32[]{:S(2)}, u32[]{:S(2)}) async-start(bf16[4,256,512]{2,1,0:T(8,128)(2,1)} %bitcast.125), calls=%async_computation.6 | async-start | bytes 2097152 | tf_op jit(solution)/shard_map/all_to_all | solution.py:109
  654.6 21.7 %collective-permute-start.44 = (bf16[128,1408]{1,0:T(8,128)(2,1)}, bf16[128,1408]{1,0:T(8,128)(2,1)}, u32[]{:S(2)}, u32[]{:S(2)}) collective-permute-start(bf16[128,1408]{1,0:T(8,128)(2,1)} %constant_dynamic-slice_fusion.17), channel_id=1, source_target_pairs={{0,8},{8,0},{1,9},{9,1},{2,10},{10,2},{3,11},{11,3},{4,12},{12,4},... | collective-permute-start | bytes 1081352 | tf_op jit(solution)/shard_map/ppermute | solution.py:50
  671.3 28.7 %all-to-all-start.9 = ((bf16[4,256,512]{2,1,0:T(8,128)(2,1)}), bf16[4,256,512]{2,1,0:T(8,128)(2,1)S(1)}, u32[]{:S(2)}, u32[]{:S(2)}) async-start(bf16[4,256,512]{2,1,0:T(8,128)(2,1)} %maximum_maximum_fusion.1), calls=%async_computation.9 | async-start | bytes 2097152 | tf_op jit(solution)/shard_map/all_to_all | solution.py:81
  700.9 38.2 %all-to-all-start.7 = ((bf16[4,288,640]{2,1,0:T(8,128)(2,1)}), bf16[4,288,640]{2,1,0:T(8,128)(2,1)S(1)}, u32[]{:S(2)}, u32[]{:S(2)}) async-start(bf16[4,288,640]{2,1,0:T(8,128)(2,1)} %pad_maximum_fusion.12), calls=%async_computation.7 | async-start | bytes 2949120 | tf_op jit(solution)/shard_map/all_to_all | solution.py:81
  712.3 30.8 %collective-permute-start.42 = (bf16[4,256,512]{2,1,0:T(8,128)(2,1)}, bf16[4,256,512]{2,1,0:T(8,128)(2,1)}, u32[]{:S(2)}, u32[]{:S(2)}) collective-permute-start(bf16[4,256,512]{2,1,0:T(8,128)(2,1)} %broadcast_select_fusion), channel_id=1, source_target_pairs={{0,16},{16,0},{1,17},{17,1},{2,18},{18,2},{3,19},{19,3},{4,20},{20... | collective-permute-start | bytes 3145736 | tf_op jit(solution)/shard_map/ppermute | solution.py:104
  (242 other events, 2493.9 us)
